TPU v7x, 32 devices: a whole 2x2x4 slice. The times are simulated.
32 devices in a mesh: roll: 4 (over x, core), tp: 8 (over z, y).
Axes of the slice: x: 2, y: 2, z: 4, core: 2. Of those that a mesh axis runs over, the one named last changes fastest.
Arguments:
- tokens: bfloat16 [128, 8, 2048], P(('roll', 'tp')), may hold values from -6 to 6
- lengths: int32 [128], P(('roll', 'tp')), may hold values from 1 to 8
- plan: int32 [2, 128, 1], P(None, ('roll', 'tp')), may hold values from 0 to 3, as said below
- owners: int32 [4], replicated, may hold values from 0 to 3, each once
- gate_up: float32 [4, 8, 2048, 768], P('roll', 'tp'), may hold values from -0.125 to 0.125
- down: float32 [4, 8, 384, 2048], P('roll', 'tp'), may hold values from -0.3125 to 0.3125
- norm_gain: float32 [2, 2048], replicated, may hold values from 0.5 to 1.5
- routing: int32 [2, 2048, 1], P(None, ('roll', 'tp')), may hold values from 0 to 7; in each aligned block of 64 rows (0 to 63, 64 to 127, ..., all dimensions but the last counted through in order) at most 10 rows name the same one
- route_weight: float32 [2, 2048], P(None, ('roll', 'tp')), may hold values from 0.1 to 1
Outputs:
- result: bfloat16 [128, 8, 2048], P(('roll', 'tp'))
Inputs may be any that keep to these rules, and one draw needn't show every extreme that they name: In layer 0 at most 2 rows of one device name the same owner, and every device's rows reach 2. For l >= 1, plan[l, i, 0] = (r + s_l[plan[l - 1, i, 0]]) mod 4, with r the roll index of row i's device and s_l a permutation of the owners drawn for layer l. owners is a permutation; layer l's master lies in the slot of roll index owners[l]. `routing`: every received token slot, empty ones included, names one window expert; of the 64 slots of one device at most 10 name the same expert, and in every draw some device reaches 10.
All inputs are finite; a program needn't handle non-finite values.
Results may differ from a plain program's by a relative error of at most 0.0048.
Values may be sent and summed in bfloat16 or wider, within the bound.
A program may use at most 128 MiB of HBM per device.

v0:
```python
import jax
import jax.numpy as jnp
from jax import lax
from jax.sharding import PartitionSpec as P

CAP = 2


epsilon = 1e-06


def spread(block, axis, owner):
    block = jnp.where(lax.axis_index(axis) == owner, block, jnp.zeros_like(block))
    return lax.psum(block, axis)


def slot_plan(target, groups, capacity):
    onehot = (target[:, None] == jnp.arange(groups, dtype=jnp.int32)[None, :]).astype(jnp.int32)
    before = jnp.cumsum(onehot, axis=0) - onehot
    within = jnp.sum(before * onehot, axis=1)
    target_slot = target * capacity + within
    item_count = target.shape[0]
    source = (
        jnp.zeros((groups * capacity,), jnp.int32)
        .at[target_slot]
        .set(jnp.arange(item_count, dtype=jnp.int32))
    )
    filled = jnp.zeros((groups * capacity,), jnp.bool_).at[target_slot].set(True)
    return (target_slot, source, filled)


def fetch_layer(gate_up, down, owners, layer_index):
    local_slot = (gate_up[0, 0].astype(jnp.bfloat16), down[0, 0].astype(jnp.bfloat16))
    return (
        spread(local_slot[0], "roll", owners[layer_index]),
        spread(local_slot[1], "roll", owners[layer_index]),
    )


def send_rows_out(current, meta_rows, source, filled, roll_size):
    row_tokens = current.shape[1]
    model_width = current.shape[2]
    send_rows = jnp.where(filled[:, None, None], current[source], jnp.zeros((), current.dtype))
    send_rows = send_rows.reshape(roll_size, CAP, row_tokens, model_width)
    send_meta = jnp.where(filled[:, None], meta_rows[source], -1)
    send_meta = send_meta.reshape(roll_size, CAP, meta_rows.shape[1])
    got_rows, got_meta = (
        lax.all_to_all(send_rows, "roll", split_axis=0, concat_axis=0, tiled=True),
        lax.all_to_all(send_meta, "roll", split_axis=0, concat_axis=0, tiled=True),
    )
    return (got_rows.reshape(-1, row_tokens, model_width), got_meta.reshape(-1, meta_rows.shape[1]))


def send_home(combined, target_slot, roll_size):
    row_tokens = combined.shape[1]
    model_width = combined.shape[2]
    home_rows = lax.all_to_all(
        combined.reshape(roll_size, CAP, row_tokens, model_width),
        "roll",
        split_axis=0,
        concat_axis=0,
        tiled=True,
    )
    return home_rows.reshape(roll_size * CAP, row_tokens, model_width)[target_slot]


def process_rows(held, held_lengths, weights, layer_gain, route_column, weight_column):
    tp_size = lax.axis_size("tp")
    row_tokens = held.shape[1]
    model_width = held.shape[2]
    received = held.reshape(-1, model_width)
    token_count = received.shape[0]
    present = (jnp.arange(row_tokens)[None, :] < held_lengths[:, None]).reshape(-1)
    widened = received.astype(jnp.float32)
    normed = (
        widened
        * lax.rsqrt(jnp.mean(widened * widened, axis=1, keepdims=True) + epsilon)
        * layer_gain[None, :]
    ).astype(jnp.bfloat16)
    expert_slots = 5 * token_count // (4 * tp_size)
    expert_target, expert_source, expert_filled = slot_plan(route_column, tp_size, expert_slots)
    send_tokens = jnp.where(
        expert_filled[:, None], normed[expert_source], jnp.zeros((), normed.dtype)
    )
    send_tokens = send_tokens.reshape(tp_size, expert_slots, model_width)
    gate_up_w, down_w = weights
    hidden_width = down_w.shape[0]
    arrived = lax.all_to_all(send_tokens, "tp", split_axis=0, concat_axis=0, tiled=True)
    flattened = arrived.reshape(-1, model_width)
    projected = jnp.dot(flattened, gate_up_w, preferred_element_type=jnp.float32)
    hidden = (jax.nn.silu(projected[:, :hidden_width]) * projected[:, hidden_width:]).astype(
        jnp.bfloat16
    )
    produced = jnp.dot(hidden, down_w, preferred_element_type=jnp.float32).astype(jnp.bfloat16)
    returned = lax.all_to_all(
        produced.reshape(arrived.shape), "tp", split_axis=0, concat_axis=0, tiled=True
    )
    answer = returned.reshape(-1, model_width)[expert_target]
    combined = (
        widened
        + (present.astype(jnp.float32) * weight_column)[:, None] * answer.astype(jnp.float32)
    ).astype(jnp.bfloat16)
    return combined.reshape(held.shape)


def per_device(tokens, lengths, plan, owners, gate_up, down, norm_gain, routing, route_weight):
    layer_count = plan.shape[0]
    roll_size = lax.axis_size("roll")
    plans = [
        slot_plan(plan[layer_index, :, 0], roll_size, CAP) for layer_index in range(layer_count)
    ]
    current = tokens
    for layer_index in range(layer_count):
        held, held_meta = send_rows_out(
            current, lengths[:, None], plans[layer_index][1], plans[layer_index][2], roll_size
        )
        combined = process_rows(
            held,
            held_meta[:, 0],
            fetch_layer(gate_up, down, owners, layer_index),
            norm_gain[layer_index],
            routing[layer_index, :, 0],
            route_weight[layer_index],
        )
        current = send_home(combined, plans[layer_index][0], roll_size)
    return current


def solution(mesh):
    in_specs = (
        P(("roll", "tp"), None, None),
        P(("roll", "tp")),
        P(None, ("roll", "tp"), None),
        P(),
        P("roll", "tp", None, None),
        P("roll", "tp", None, None),
        P(),
        P(None, ("roll", "tp"), None),
        P(None, ("roll", "tp")),
    )
    out_specs = P(("roll", "tp"), None, None)
    return jax.shard_map(
        per_device, mesh=mesh, in_specs=in_specs, out_specs=out_specs, check_vma=False
    )
```

profile of v0, /device:TPU:0, one launch (start us, length us, event | category | flops | bytes accessed | tf_op | source)
XLA Modules:
  0.0 311.0 jit_solution(11454669175080193429)
XLA Ops:
  9.3 3.9 %select_bitcast_fusion.3 = (bf16[384,2048]{1,0:T(8,128)(2,1)}, bf16[384,2048]{1,0:T(8,128)(2,1)}) fusion(pred[]{:T(512)S(6)} %eq.80, f32[1,1,384,2048]{3,2,1,0:T(8,128)} %param.14, pred[]{:T(512)S(6)} %eq.85), kind=kLoop, calls=%fused_computation.23 | loop fusion | flops 2359296 | bytes 6291458 | tf_op jit(solution)/shard_map/jit(_where)/select_n | solution.py:13
  14.1 3.1 select_bitcast_fusion
  21.0 4.2 %all-to-all-start = ((bf16[4,2,8,2048]{3,2,1,0:T(8,128)(2,1)}), bf16[4,2,8,2048]{3,2,1,0:T(8,128)(2,1)S(1)}, u32[]{:S(2)}, u32[]{:S(2)}) async-start(bf16[4,2,8,2048]{3,2,1,0:T(8,128)(2,1)} %broadcast_select_fusion.2), calls=%async_computation | async-start | bytes 524288 | tf_op jit(solution)/shard_map/all_to_all | solution.py:48
  27.5 6.7 %all-to-all-done = bf16[4,2,8,2048]{3,2,1,0:T(8,128)(2,1)S(1)} async-done(((bf16[4,2,8,2048]{3,2,1,0:T(8,128)(2,1)}), bf16[4,2,8,2048]{3,2,1,0:T(8,128)(2,1)S(1)}, u32[]{:S(2)}, u32[]{:S(2)}) %all-to-all-start) | async-done | bytes 262176 | tf_op jit(solution)/shard_map/all_to_all | solution.py:48
  36.4 6.6 %all-to-all-start.2 = ((bf16[8,10,2048]{2,1,0:T(8,128)(2,1)}), bf16[8,10,2048]{2,1,0:T(8,128)(2,1)S(1)}, u32[]{:S(2)}, u32[]{:S(2)}) async-start(bf16[8,10,2048]{2,1,0:T(8,128)(2,1)} %broadcast_select_fusion.1), calls=%async_computation.2 | async-start | bytes 1048576 | tf_op jit(solution)/shard_map/all_to_all | solution.py:88
  44.4 13.0 %all-to-all-done.2 = bf16[8,10,2048]{2,1,0:T(8,128)(2,1)S(1)} async-done(((bf16[8,10,2048]{2,1,0:T(8,128)(2,1)}), bf16[8,10,2048]{2,1,0:T(8,128)(2,1)S(1)}, u32[]{:S(2)}, u32[]{:S(2)}) %all-to-all-start.2) | async-done | bytes 327712 | tf_op jit(solution)/shard_map/all_to_all | solution.py:88
  57.4 3.2 %all-to-all-start.1 = ((s32[4,2,1]{1,2,0:T(1,128)}), s32[4,2,1]{1,2,0:T(1,128)S(1)}, u32[]{:S(2)}, u32[]{:S(2)}) async-start(s32[4,2,1]{1,2,0:T(1,128)} %bitcast.9), calls=%async_computation.1 | async-start | bytes 4096 | tf_op jit(solution)/shard_map/all_to_all | solution.py:49
  60.7 133.1 %all-reduce.3.cloned.1.call-done = (bf16[384,2048]{1,0:T(8,128)(2,1)}, bf16[384,2048]{1,0:T(8,128)(2,1)}, bf16[2048,768]{1,0:T(8,128)(2,1)}, bf16[2048,768]{1,0:T(8,128)(2,1)}) async-done(((bf16[384,2048]{1,0:T(8,128)(2,1)}, bf16[384,2048]{1,0:T(8,128)(2,1)}, bf16[2048,768]{1,0:T(8,128)(2,1)}, bf16[2048,768]{1,0:T(8,128)(2,1)}), (bf16[384,2048]{1,0:T(8,128)(2,1)}, bf16[384,2048]{1,0:T(8,128)(2,1)}, ...) | async-done | bytes 9437200 | tf_op jit(solution)/shard_map/psum | solution.py:14
  193.8 2.7 fusion.42
  197.8 5.5 %all-to-all-start.3 = ((bf16[8,10,2048]{2,1,0:T(8,128)(2,1)}), bf16[8,10,2048]{2,1,0:T(8,128)(2,1)S(1)}, u32[]{:S(2)}, u32[]{:S(2)}) async-start(bf16[8,10,2048]{2,1,0:T(8,128)(2,1)} %reshape.292), calls=%async_computation.3 | async-start | bytes 1048576 | tf_op jit(solution)/shard_map/all_to_all | solution.py:95
  206.2 11.5 %all-to-all-done.3 = bf16[8,10,2048]{2,1,0:T(8,128)(2,1)S(1)} async-done(((bf16[8,10,2048]{2,1,0:T(8,128)(2,1)}), bf16[8,10,2048]{2,1,0:T(8,128)(2,1)S(1)}, u32[]{:S(2)}, u32[]{:S(2)}) %all-to-all-start.3) | async-done | bytes 327712 | tf_op jit(solution)/shard_map/all_to_all | solution.py:95
  219.4 3.4 %all-to-all-start.4 = ((bf16[4,2,8,2048]{3,2,1,0:T(8,128)(2,1)}), bf16[4,2,8,2048]{3,2,1,0:T(8,128)(2,1)S(1)}, u32[]{:S(2)}, u32[]{:S(2)}) async-start(bf16[4,2,8,2048]{3,2,1,0:T(8,128)(2,1)} %fusion.3), calls=%async_computation.4 | async-start | bytes 524288 | tf_op jit(solution)/shard_map/all_to_all | solution.py:57
  222.9 6.0 %all-to-all-done.4 = bf16[4,2,8,2048]{3,2,1,0:T(8,128)(2,1)S(1)} async-done(((bf16[4,2,8,2048]{3,2,1,0:T(8,128)(2,1)}), bf16[4,2,8,2048]{3,2,1,0:T(8,128)(2,1)S(1)}, u32[]{:S(2)}, u32[]{:S(2)}) %all-to-all-start.4) | async-done | bytes 262176 | tf_op jit(solution)/shard_map/all_to_all | solution.py:57
  230.8 3.4 %all-to-all-start.5 = ((bf16[4,2,8,2048]{3,2,1,0:T(8,128)(2,1)}), bf16[4,2,8,2048]{3,2,1,0:T(8,128)(2,1)S(1)}, u32[]{:S(2)}, u32[]{:S(2)}) async-start(bf16[4,2,8,2048]{3,2,1,0:T(8,128)(2,1)} %broadcast_select_fusion.3), calls=%async_computation.5 | async-start | bytes 524288 | tf_op jit(solution)/shard_map/all_to_all | solution.py:48
  235.6 4.5 %all-to-all-done.5 = bf16[4,2,8,2048]{3,2,1,0:T(8,128)(2,1)S(1)} async-done(((bf16[4,2,8,2048]{3,2,1,0:T(8,128)(2,1)}), bf16[4,2,8,2048]{3,2,1,0:T(8,128)(2,1)S(1)}, u32[]{:S(2)}, u32[]{:S(2)}) %all-to-all-start.5) | async-done | bytes 262176 | tf_op jit(solution)/shard_map/all_to_all | solution.py:48
  242.1 2.0 gather.55
  244.1 2.0 broadcast_select_fusion
  246.1 4.1 %all-to-all-start.7 = ((bf16[8,10,2048]{2,1,0:T(8,128)(2,1)}), bf16[8,10,2048]{2,1,0:T(8,128)(2,1)}, u32[]{:S(2)}, u32[]{:S(2)}) async-start(bf16[8,10,2048]{2,1,0:T(8,128)(2,1)} %broadcast_select_fusion), calls=%async_computation.7 | async-start | bytes 1048576 | tf_op jit(solution)/shard_map/all_to_all | solution.py:88
  252.7 12.1 %all-to-all-done.7 = bf16[8,10,2048]{2,1,0:T(8,128)(2,1)} async-done(((bf16[8,10,2048]{2,1,0:T(8,128)(2,1)}), bf16[8,10,2048]{2,1,0:T(8,128)(2,1)}, u32[]{:S(2)}, u32[]{:S(2)}) %all-to-all-start.7) | async-done | bytes 327712 | tf_op jit(solution)/shard_map/all_to_all | solution.py:88
  264.8 3.2 %all-to-all-start.6 = ((s32[4,2,1]{1,2,0:T(1,128)}), s32[4,2,1]{1,2,0:T(1,128)S(1)}, u32[]{:S(2)}, u32[]{:S(2)}) async-start(s32[4,2,1]{1,2,0:T(1,128)} %bitcast.23), calls=%async_computation.6 | async-start | bytes 4096 | tf_op jit(solution)/shard_map/all_to_all | solution.py:49
  273.0 3.6 %all-to-all-start.8 = ((bf16[8,10,2048]{2,1,0:T(8,128)(2,1)}), bf16[8,10,2048]{2,1,0:T(8,128)(2,1)S(1)}, u32[]{:S(2)}, u32[]{:S(2)}) async-start(bf16[8,10,2048]{2,1,0:T(8,128)(2,1)} %reshape.297), calls=%async_computation.8 | async-start | bytes 1048576 | tf_op jit(solution)/shard_map/all_to_all | solution.py:95
  276.8 15.0 %all-to-all-done.8 = bf16[8,10,2048]{2,1,0:T(8,128)(2,1)S(1)} async-done(((bf16[8,10,2048]{2,1,0:T(8,128)(2,1)}), bf16[8,10,2048]{2,1,0:T(8,128)(2,1)S(1)}, u32[]{:S(2)}, u32[]{:S(2)}) %all-to-all-start.8) | async-done | bytes 327712 | tf_op jit(solution)/shard_map/all_to_all | solution.py:95
  293.5 3.4 %all-to-all-start.9 = ((bf16[4,2,8,2048]{3,2,1,0:T(8,128)(2,1)}), bf16[4,2,8,2048]{3,2,1,0:T(8,128)(2,1)S(1)}, u32[]{:S(2)}, u32[]{:S(2)}) async-start(bf16[4,2,8,2048]{3,2,1,0:T(8,128)(2,1)} %fusion.1), calls=%async_computation.9 | async-start | bytes 524288 | tf_op jit(solution)/shard_map/all_to_all | solution.py:57
  296.9 6.0 %all-to-all-done.9 = bf16[4,2,8,2048]{3,2,1,0:T(8,128)(2,1)S(1)} async-done(((bf16[4,2,8,2048]{3,2,1,0:T(8,128)(2,1)}), bf16[4,2,8,2048]{3,2,1,0:T(8,128)(2,1)S(1)}, u32[]{:S(2)}, u32[]{:S(2)}) %all-to-all-start.9) | async-done | bytes 262176 | tf_op jit(solution)/shard_map/all_to_all | solution.py:57
  (116 shorter events, 33.5 us)
Async XLA Ops:
  6.5 13.1 %copy-start = (bf16[4,8,2048]{2,1,0:T(8,128)(2,1)S(1)}, bf16[4,8,2048]{2,1,0:T(8,128)(2,1)}, u32[]{:S(2)}) copy-start(bf16[4,8,2048]{2,1,0:T(8,128)(2,1)} %param.9) | copy-start | bytes 393220
  6.5 187.3 %all-reduce.3.cloned.1.call-start = ((), (), s32[]{:S(2)}) async-start(), calls=%async_computation.10 | async-start | bytes 18874368 | tf_op jit(solution)/shard_map/psum | solution.py:14
  9.3 4.9 %copy-start.2 = (f32[1,1,2048,768]{3,2,1,0:T(8,128)S(1)}, f32[1,1,2048,768]{3,2,1,0:T(8,128)}, u32[]{:S(2)}) copy-start(f32[1,1,2048,768]{3,2,1,0:T(8,128)} %param.13) | copy-start | bytes 18874372
  17.2 0.7 copy-start.7
  17.2 8.0 %copy-start.8 = (s32[2,64,1]{1,2,0:T(1,128)S(1)}, s32[2,64,1]{1,2,0:T(1,128)}, u32[]{:S(2)}) copy-start(s32[2,64,1]{1,2,0:T(1,128)} %param.16) | copy-start | bytes 1540
  17.2 9.4 %copy-start.6 = (f32[2,2048]{1,0:T(2,128)S(1)}, f32[2,2048]{1,0:T(2,128)}, u32[]{:S(2)}) copy-start(f32[2,2048]{1,0:T(2,128)} %param.15) | copy-start | bytes 49156
  21.0 13.2 %all-to-all-start = ((bf16[4,2,8,2048]{3,2,1,0:T(8,128)(2,1)}), bf16[4,2,8,2048]{3,2,1,0:T(8,128)(2,1)S(1)}, u32[]{:S(2)}, u32[]{:S(2)}) async-start(bf16[4,2,8,2048]{3,2,1,0:T(8,128)(2,1)} %broadcast_select_fusion.2), calls=%async_computation | async-start | bytes 524288 | tf_op jit(solution)/shard_map/all_to_all | solution.py:48
  34.5 8.5 %copy-start.1 = (s32[4]{0:T(128)S(1)}, s32[4]{0:T(128)}, u32[]{:S(2)}) copy-start(s32[4]{0:T(128)} %param.10) | copy-start | bytes 52
  36.4 20.9 %all-to-all-start.2 = ((bf16[8,10,2048]{2,1,0:T(8,128)(2,1)}), bf16[8,10,2048]{2,1,0:T(8,128)(2,1)S(1)}, u32[]{:S(2)}, u32[]{:S(2)}) async-start(bf16[8,10,2048]{2,1,0:T(8,128)(2,1)} %broadcast_select_fusion.1), calls=%async_computation.2 | async-start | bytes 1048576 | tf_op jit(solution)/shard_map/all_to_all | solution.py:88
  57.4 140.5 %all-to-all-start.1 = ((s32[4,2,1]{1,2,0:T(1,128)}), s32[4,2,1]{1,2,0:T(1,128)S(1)}, u32[]{:S(2)}, u32[]{:S(2)}) async-start(s32[4,2,1]{1,2,0:T(1,128)} %bitcast.9), calls=%async_computation.1 | async-start | bytes 4096 | tf_op jit(solution)/shard_map/all_to_all | solution.py:49
  193.8 2.7 copy-start.5
  193.8 9.5 %copy-start.10 = (f32[2,64]{1,0:T(2,128)S(1)}, f32[2,64]{1,0:T(2,128)}, u32[]{:S(2)}) copy-start(f32[2,64]{1,0:T(2,128)} %param.17) | copy-start | bytes 1540
  197.8 19.9 %all-to-all-start.3 = ((bf16[8,10,2048]{2,1,0:T(8,128)(2,1)}), bf16[8,10,2048]{2,1,0:T(8,128)(2,1)S(1)}, u32[]{:S(2)}, u32[]{:S(2)}) async-start(bf16[8,10,2048]{2,1,0:T(8,128)(2,1)} %reshape.292), calls=%async_computation.3 | async-start | bytes 1048576 | tf_op jit(solution)/shard_map/all_to_all | solution.py:95
  204.6 1.5 copy-start.11
  219.4 9.4 %all-to-all-start.4 = ((bf16[4,2,8,2048]{3,2,1,0:T(8,128)(2,1)}), bf16[4,2,8,2048]{3,2,1,0:T(8,128)(2,1)S(1)}, u32[]{:S(2)}, u32[]{:S(2)}) async-start(bf16[4,2,8,2048]{3,2,1,0:T(8,128)(2,1)} %fusion.3), calls=%async_computation.4 | async-start | bytes 524288 | tf_op jit(solution)/shard_map/all_to_all | solution.py:57
  230.8 9.4 %all-to-all-start.5 = ((bf16[4,2,8,2048]{3,2,1,0:T(8,128)(2,1)}), bf16[4,2,8,2048]{3,2,1,0:T(8,128)(2,1)S(1)}, u32[]{:S(2)}, u32[]{:S(2)}) async-start(bf16[4,2,8,2048]{3,2,1,0:T(8,128)(2,1)} %broadcast_select_fusion.3), calls=%async_computation.5 | async-start | bytes 524288 | tf_op jit(solution)/shard_map/all_to_all | solution.py:48
  242.1 27.8 %copy-start.3 = (bf16[2048,768]{1,0:T(8,128)(2,1)S(1)}, bf16[2048,768]{1,0:T(8,128)(2,1)}, u32[]{:S(2)}) copy-start(bf16[2048,768]{1,0:T(8,128)(2,1)} %get-tuple-element.10) | copy-start | bytes 9437188
  246.1 18.7 %all-to-all-start.7 = ((bf16[8,10,2048]{2,1,0:T(8,128)(2,1)}), bf16[8,10,2048]{2,1,0:T(8,128)(2,1)}, u32[]{:S(2)}, u32[]{:S(2)}) async-start(bf16[8,10,2048]{2,1,0:T(8,128)(2,1)} %broadcast_select_fusion), calls=%async_computation.7 | async-start | bytes 1048576 | tf_op jit(solution)/shard_map/all_to_all | solution.py:88
  264.8 8.2 %all-to-all-start.6 = ((s32[4,2,1]{1,2,0:T(1,128)}), s32[4,2,1]{1,2,0:T(1,128)S(1)}, u32[]{:S(2)}, u32[]{:S(2)}) async-start(s32[4,2,1]{1,2,0:T(1,128)} %bitcast.23), calls=%async_computation.6 | async-start | bytes 4096 | tf_op jit(solution)/shard_map/all_to_all | solution.py:49
  269.9 1.7 copy-start.4
  269.9 6.7 %copy-start.9 = (f32[64]{0:T(128)S(1)}, f32[64]{0:T(128)}, u32[]{:S(2)}) copy-start(f32[64]{0:T(128)} %get-tuple-element.5) | copy-start | bytes 772
  273.0 18.8 %all-to-all-start.8 = ((bf16[8,10,2048]{2,1,0:T(8,128)(2,1)}), bf16[8,10,2048]{2,1,0:T(8,128)(2,1)S(1)}, u32[]{:S(2)}, u32[]{:S(2)}) async-start(bf16[8,10,2048]{2,1,0:T(8,128)(2,1)} %reshape.297), calls=%async_computation.8 | async-start | bytes 1048576 | tf_op jit(solution)/shard_map/all_to_all | solution.py:95
  293.5 9.4 %all-to-all-start.9 = ((bf16[4,2,8,2048]{3,2,1,0:T(8,128)(2,1)}), bf16[4,2,8,2048]{3,2,1,0:T(8,128)(2,1)S(1)}, u32[]{:S(2)}, u32[]{:S(2)}) async-start(bf16[4,2,8,2048]{3,2,1,0:T(8,128)(2,1)} %fusion.1), calls=%async_computation.9 | async-start | bytes 524288 | tf_op jit(solution)/shard_map/all_to_all | solution.py:57
Sparse Core Ops, SparseCore 0:
  17.4 176.4 all-reduce.2
where the time goes:
time: 312 us; the launch traced here: 311 us
  waiting for transfers between devices  208 us (67%)
  starting transfers between devices  40.7 us (13%)
  local copies, waits for them, and re-layouts  26.3 us (8%)
  other arithmetic  15.6 us (5%)
  between operations  15.1 us (5%)
  matrix products  5.22 us (2%)
    psum x1, waiting for transfers between devices, spread(): return lax.psum(block, axis)  133 us
    all_to_all x2, waiting for transfers between devices, process_rows(): lax.all_to_all(produced.reshape(arrived.shape), 'tp', split_axis=0, conca...  26.5 us
    all_to_all x2, waiting for transfers between devices, process_rows(): lax.all_to_all(send_tokens, 'tp', split_axis=0, concat_axis=0, tiled=True)  25.1 us
    all_to_all x2, waiting for transfers between devices, send_home(): lax.all_to_all(combined.reshape(roll_size, CAP, row_tokens, model_width),...  12 us
    all_to_all x2, waiting for transfers between devices, send_rows_out(): lax.all_to_all(send_rows, 'roll', split_axis=0, concat_axis=0, tiled=True)  11.3 us
    all_to_all x2, starting transfers between devices, process_rows(): lax.all_to_all(send_tokens, 'tp', split_axis=0, concat_axis=0, tiled=True)  10.7 us
    all_to_all x2, starting transfers between devices, process_rows(): lax.all_to_all(produced.reshape(arrived.shape), 'tp', split_axis=0, conca...  9.14 us
    all_to_all x2, starting transfers between devices, send_rows_out(): lax.all_to_all(send_rows, 'roll', split_axis=0, concat_axis=0, tiled=True)  7.61 us
  transfers between devices with their start and end apart: 11, of which 9 were waited for; matrix products, arithmetic and copies ran while one was open for 8% of the time, Pallas kernels for 0%

commit v1 on v0

v1 whole, which is shorter than its diff:
```python
import jax
import jax.numpy as jnp
from jax import lax
from jax.sharding import PartitionSpec as P

CAP = 2


epsilon = 1e-06


def spread(block, axis, owner):
    block = jnp.where(lax.axis_index(axis) == owner, block, jnp.zeros_like(block))
    return lax.psum(block, axis)


def slot_plan(target, groups, capacity):
    count = target.shape[0]
    earlier = jnp.arange(count)[None, :] < jnp.arange(count)[:, None]
    same = target[:, None] == target[None, :]
    within = jnp.sum(jnp.logical_and(same, earlier).astype(jnp.int32), axis=1)
    slot = target * capacity + within
    return (jnp.arange(groups * capacity)[:, None] == slot[None, :]).astype(jnp.bfloat16)


def into_slots(taken, items):
    flat = items.reshape(items.shape[0], -1)
    placed = jnp.dot(taken, flat, preferred_element_type=jnp.float32).astype(items.dtype)
    return placed.reshape((-1,) + items.shape[1:])


def from_slots(taken, slots):
    return into_slots(taken.T, slots)


def fetch_layer(gate_up, down, owners, layer_index):
    local_slot = (gate_up[0, 0].astype(jnp.bfloat16), down[0, 0].astype(jnp.bfloat16))
    return (
        spread(local_slot[0], "roll", owners[layer_index]),
        spread(local_slot[1], "roll", owners[layer_index]),
    )


def send_rows_out(current, lengths, taken):
    got_rows = lax.all_to_all(into_slots(taken, current), "roll", split_axis=0, concat_axis=0, tiled=True)
    send_lengths = jnp.sum(jnp.where(taken > 0, lengths[None, :], 0), axis=1)
    got_lengths = lax.all_to_all(send_lengths[:, None], "roll", split_axis=0, concat_axis=0, tiled=True)
    return (got_rows, got_lengths[:, 0])


def send_home(combined, taken):
    home_rows = lax.all_to_all(combined, "roll", split_axis=0, concat_axis=0, tiled=True)
    return from_slots(taken, home_rows)


def process_rows(held, held_lengths, weights, layer_gain, route_column, weight_column):
    tp_size = lax.axis_size("tp")
    row_tokens = held.shape[1]
    model_width = held.shape[2]
    received = held.reshape(-1, model_width)
    token_count = received.shape[0]
    present = (jnp.arange(row_tokens)[None, :] < held_lengths[:, None]).reshape(-1)
    widened = received.astype(jnp.float32)
    normed = (
        widened
        * lax.rsqrt(jnp.mean(widened * widened, axis=1, keepdims=True) + epsilon)
        * layer_gain[None, :]
    ).astype(jnp.bfloat16)
    expert_slots = 5 * token_count // (4 * tp_size)
    taken = slot_plan(route_column, tp_size, expert_slots)
    send_tokens = into_slots(taken, normed).reshape(tp_size, expert_slots, model_width)
    gate_up_w, down_w = weights
    hidden_width = down_w.shape[0]
    arrived = lax.all_to_all(send_tokens, "tp", split_axis=0, concat_axis=0, tiled=True)
    flattened = arrived.reshape(-1, model_width)
    projected = jnp.dot(flattened, gate_up_w, preferred_element_type=jnp.float32)
    hidden = (jax.nn.silu(projected[:, :hidden_width]) * projected[:, hidden_width:]).astype(
        jnp.bfloat16
    )
    produced = jnp.dot(hidden, down_w, preferred_element_type=jnp.float32).astype(jnp.bfloat16)
    returned = lax.all_to_all(
        produced.reshape(arrived.shape), "tp", split_axis=0, concat_axis=0, tiled=True
    )
    answer = from_slots(taken, returned.reshape(-1, model_width))
    combined = (
        widened
        + (present.astype(jnp.float32) * weight_column)[:, None] * answer.astype(jnp.float32)
    ).astype(jnp.bfloat16)
    return combined.reshape(held.shape)


def per_device_wide(tokens, lengths, plan, owners, gate_up, down, norm_gain, routing, route_weight):
    layer_count = plan.shape[0]
    roll_size = lax.axis_size("roll")
    plans = [
        slot_plan(plan[layer_index, :, 0], roll_size, CAP) for layer_index in range(layer_count)
    ]
    current = tokens
    for layer_index in range(layer_count):
        held, held_lengths = send_rows_out(current, lengths, plans[layer_index])
        combined = process_rows(
            held,
            held_lengths,
            fetch_layer(gate_up, down, owners, layer_index),
            norm_gain[layer_index],
            routing[layer_index, :, 0],
            route_weight[layer_index],
        )
        current = send_home(combined, plans[layer_index])
    return current


GATHER_LIMIT = 1 << 23


def token_tables(plan, routing, route_weight, row_tokens, roll_size, tp_size):
    layer_count, rows_dev = plan.shape[0], plan.shape[1]
    slots = routing.shape[1]
    packed = jnp.concatenate(
        [
            plan[:, :, 0].astype(jnp.float32).reshape(-1),
            routing[:, :, 0].astype(jnp.float32).reshape(-1),
            route_weight.reshape(-1),
        ]
    )
    everyone = lax.all_gather(packed, ("roll", "tp"))
    first, second = layer_count * rows_dev, layer_count * (rows_dev + slots)
    owner = everyone[:, :first].reshape(roll_size, tp_size, layer_count, rows_dev)
    owner = owner.astype(jnp.int32).transpose(2, 0, 1, 3)

    def table_of(part):
        part = part.reshape(roll_size, tp_size, layer_count, roll_size, CAP, row_tokens)
        return part.transpose(2, 3, 1, 0, 4, 5)

    expert_table = table_of(everyone[:, first:second])
    weight_table = table_of(everyone[:, second:])
    earlier = jnp.arange(rows_dev)[None, :] < jnp.arange(rows_dev)[:, None]
    same = owner[..., :, None] == owner[..., None, :]
    within = jnp.sum(jnp.logical_and(same, earlier).astype(jnp.int32), axis=-1)
    picks = jnp.logical_and(
        owner[..., None, None] == jnp.arange(roll_size)[:, None],
        within[..., None, None] == jnp.arange(CAP)[None, :],
    )

    def pick(table):
        kept = jnp.where(picks[..., None], table[:, :, :, None], 0.0)
        return jnp.sum(kept, axis=(-3, -2))

    return pick(expert_table).astype(jnp.int32), pick(weight_table)


def per_device_gathered(tokens, lengths, plan, owners, gate_up, down, norm_gain, routing, route_weight):
    layer_count = plan.shape[0]
    roll_size, tp_size = lax.axis_size("roll"), lax.axis_size("tp")
    rows_dev, row_tokens, model_width = tokens.shape
    my_roll, my_tp = lax.axis_index("roll"), lax.axis_index("tp")
    experts, scales = token_tables(plan, routing, route_weight, row_tokens, roll_size, tp_size)
    scales = scales[:, my_roll, my_tp].reshape(layer_count, -1)
    present = (jnp.arange(row_tokens)[None, :] < lengths[:, None]).astype(jnp.float32).reshape(-1)
    gate_up_w, down_w = gate_up[0, 0].astype(jnp.bfloat16), down[0, 0].astype(jnp.bfloat16)
    hidden_width = down_w.shape[0]
    current = tokens.reshape(-1, model_width)
    for layer in range(layer_count):
        widened = current.astype(jnp.float32)
        normed = (
            widened
            * lax.rsqrt(jnp.mean(widened * widened, axis=1, keepdims=True) + epsilon)
            * norm_gain[layer][None, :]
        ).astype(jnp.bfloat16)
        arrived = lax.all_gather(normed, ("roll", "tp"), tiled=True)
        projected = jnp.dot(arrived, gate_up_w, preferred_element_type=jnp.float32)
        hidden = (jax.nn.silu(projected[:, :hidden_width]) * projected[:, hidden_width:]).astype(jnp.bfloat16)
        produced = jnp.dot(hidden, down_w, preferred_element_type=jnp.float32).astype(jnp.bfloat16)
        mine = jnp.logical_and(experts[layer].reshape(-1) == my_tp, owners[layer] == my_roll)
        produced = jnp.where(mine[:, None], produced, jnp.zeros((), produced.dtype))
        answer = lax.psum_scatter(produced, ("roll", "tp"), scatter_dimension=0, tiled=True)
        current = (
            widened + (present * scales[layer])[:, None] * answer.astype(jnp.float32)
        ).astype(jnp.bfloat16)
    return current.reshape(tokens.shape)


def per_device(tokens, *rest):
    devices = lax.axis_size("roll") * lax.axis_size("tp")
    if devices * tokens.size * 2 > GATHER_LIMIT:
        return per_device_wide(tokens, *rest)
    return per_device_gathered(tokens, *rest)


def solution(mesh):
    in_specs = (
        P(("roll", "tp"), None, None),
        P(("roll", "tp")),
        P(None, ("roll", "tp"), None),
        P(),
        P("roll", "tp", None, None),
        P("roll", "tp", None, None),
        P(),
        P(None, ("roll", "tp"), None),
        P(None, ("roll", "tp")),
    )
    out_specs = P(("roll", "tp"), None, None)
    return jax.shard_map(
        per_device, mesh=mesh, in_specs=in_specs, out_specs=out_specs, check_vma=False
    )
```

time: 312 us -> 454 us (1.46)
  waiting for transfers between devices: 208 us -> 360 us
  blocking collectives: 0 us -> 42.5 us
  starting transfers between devices: 40.7 us -> 0.13 us
  local copies, waits for them, and re-layouts: 26.3 us -> 5.64 us
  matrix products: 5.22 us -> 21.9 us
  other arithmetic: 15.6 us -> 8.71 us
    reduce_scatter x0 -> x2, waiting for transfers between devices: none -> 284 us  [per_device_gathered(): lax.psum_scatter(produced, ('roll', 'tp'), scatter_dimension=0, tiled=True)]
    psum x1 -> x0, waiting for transfers between devices: 133 us -> none  [spread(): return lax.psum(block, axis)]
    all_gather x0 -> x2, waiting for transfers between devices: none -> 75.4 us  [per_device_gathered(): arrived = lax.all_gather(normed, ('roll', 'tp'), tiled=True)]
    all_to_all x10 -> x0, waiting for transfers between devices: 74.9 us -> none  [the longest x2 26.5 us: process_rows(): lax.all_to_all(produced.reshape(arrived.shape), 'tp', split_axis=0, conca...]
    unnamed x0 -> x1, blocking collectives: none -> 42.5 us
    all_to_all x10 -> x0, starting transfers between devices: 40.7 us -> none  [the longest x2 10.7 us: process_rows(): lax.all_to_all(send_tokens, 'tp', split_axis=0, concat_axis=0, tiled=True)]
    dot_general x4, matrix products: 5.22 us -> 21.9 us  [the longest x2 14.1 us: per_device_gathered(): projected = jnp.dot(arrived, gate_up_w, preferred_element_type=jnp.float32)]
    select_n x14 -> x0, other arithmetic: 12.1 us -> none  [the longest x2 6.98 us: spread(): jnp.where(lax.axis_index(axis) == owner, block, jnp.zeros_like(block))]
  transfers between devices with their start and end apart: 11 -> 4, of which waited for: 9 -> 4; matrix products, arithmetic and copies ran while one was open for 8% -> 1% of each run, Pallas kernels for 0% -> 0%
where the time goes in v1:
time: 454 us; the launch traced here: 453 us
  waiting for transfers between devices  360 us (79%)
  blocking collectives  42.5 us (9%)
  matrix products  21.9 us (5%)
  between operations  14.5 us (3%)
  other arithmetic  8.71 us (2%)
  local copies, waits for them, and re-layouts  5.64 us (1%)
    reduce_scatter x2, waiting for transfers between devices, per_device_gathered(): lax.psum_scatter(produced, ('roll', 'tp'), scatter_dimension=0, tiled=True)  284 us
    all_gather x2, waiting for transfers between devices, per_device_gathered(): arrived = lax.all_gather(normed, ('roll', 'tp'), tiled=True)  75.4 us
    unnamed x1, blocking collectives  42.5 us
    dot_general x2, matrix products, per_device_gathered(): projected = jnp.dot(arrived, gate_up_w, preferred_element_type=jnp.float32)  14.1 us
  transfers between devices with their start and end apart: 4, of which 4 were waited for; matrix products, arithmetic and copies ran while one was open for 1% of the time, Pallas kernels for 0%

profile of v1, /device:TPU:0, one launch (start us, length us, event | category | flops | bytes accessed | tf_op | source)
XLA Modules:
  0.0 453.4 jit_solution(18064298914493296082)
XLA Ops:
  6.5 1.0 fusion.21
  7.7 0.8 fusion.33
  8.5 1.7 fusion.19
  10.2 0.8 reshape.138
  11.0 0.7 convert_reduce_fusion.2
  11.8 0.7 convert_reduce_fusion.1
  12.5 1.3 fusion.34
  15.1 0.2 maximum_dynamic-update-slice_fusion
  15.3 42.5 %all-reduce = f32[8448]{0:T(1024)S(1)} all-reduce(f32[8448]{0:T(1024)S(1)} %maximum_dynamic-update-slice_fusion), channel_id=2, replica_groups=mesh['roll'=4,'tp'=8] {'roll','tp'}, use_global_device_ids=true, to_apply=%add | all-reduce | flops 8448 | bytes 67584
  58.2 0.4 reshape.140
  58.7 0.4 reshape.139
  59.6 0.5 select_reduce_fusion.1
  60.2 15.1 %all-gather.4.cloned.1.call-done = bf16[1024,2048]{1,0:T(8,128)(2,1)} async-done(((bf16[32,2048]{1,0:T(8,128)(2,1)}), bf16[1024,2048]{1,0:T(8,128)(2,1)}) %all-gather.4.cloned.1.call-update) | async-done | bytes 4194320 | tf_op jit(solution)/shard_map/all_gather | solution.py:170
  75.3 7.0 %fusion.2 = f32[1024,768]{1,0:T(8,128)S(1)} fusion(bf16[1024,2048]{1,0:T(8,128)(2,1)} %all-gather.4.cloned.1.call-done, f32[1,1,2048,768]{3,2,1,0:T(8,128)} %param.13), kind=kOutput, calls=%fused_computation.4 | convolution fusion | flops 3222798336 | bytes 13631488 | tf_op jit(solution)/shard_map/dot_general | solution.py:171
  82.4 3.9 convert_select_fusion.1
  86.3 0.6 copy-done.2
  87.3 141.8 %reduce-scatter.3.cloned.1.call-done = bf16[32,2048]{1,0:T(8,128)(2,1)} async-done(((bf16[1024,2048]{1,0:T(8,128)(2,1)}), bf16[32,2048]{1,0:T(8,128)(2,1)}) %reduce-scatter.3.cloned.1.call-update) | async-done | bytes 131088 | tf_op jit(solution)/shard_map/reduce_scatter | solution.py:176
  229.0 1.1 fusion.22
  230.2 0.8 fusion.24
  231.2 60.4 %all-gather.6.cloned.1.call-done = bf16[1024,2048]{1,0:T(8,128)(2,1)} async-done(((bf16[32,2048]{1,0:T(8,128)(2,1)}), bf16[1024,2048]{1,0:T(8,128)(2,1)}) %all-gather.6.cloned.1.call-update) | async-done | bytes 4194320 | tf_op jit(solution)/shard_map/all_gather | solution.py:170
  291.5 7.0 %fusion = f32[1024,768]{1,0:T(8,128)S(1)} fusion(bf16[1024,2048]{1,0:T(8,128)(2,1)} %all-gather.6.cloned.1.call-done, f32[1,1,2048,768]{3,2,1,0:T(8,128)} %param.13), kind=kOutput, calls=%fused_computation.2 | convolution fusion | flops 3222798336 | bytes 13631488 | tf_op jit(solution)/shard_map/dot_general | solution.py:171
  298.6 3.9 convert_select_fusion
  302.5 142.7 %reduce-scatter.5.cloned.1.call-done = bf16[32,2048]{1,0:T(8,128)(2,1)} async-done(((bf16[1024,2048]{1,0:T(8,128)(2,1)}), bf16[32,2048]{1,0:T(8,128)(2,1)}) %reduce-scatter.5.cloned.1.call-update) | async-done | bytes 131088 | tf_op jit(solution)/shard_map/reduce_scatter | solution.py:176
  445.2 1.7 fusion.26
  (45 shorter events, 1.9 us)
Async XLA Ops:
  6.5 68.8 %all-gather.4.cloned.1.call-start = ((), (), s32[]{:S(2)}) async-start(), calls=%async_computation.2 | async-start | bytes 4325376 | tf_op jit(solution)/shard_map/all_gather | solution.py:170
  10.2 218.9 %reduce-scatter.3.cloned.1.call-start = ((), (), s32[]{:S(2)}) async-start(), calls=%async_computation.3 | async-start | bytes 4325376 | tf_op jit(solution)/shard_map/reduce_scatter | solution.py:176
  60.2 22.1 %copy-start.1 = (f32[1,1,384,2048]{3,2,1,0:T(8,128)S(1)}, f32[1,1,384,2048]{3,2,1,0:T(8,128)}, u32[]{:S(2)}) copy-start(f32[1,1,384,2048]{3,2,1,0:T(8,128)} %param.14) | copy-start | bytes 9437188
  86.3 0.7 copy-start.2
  86.3 142.8 %copy-start = (bf16[4,8,2048]{2,1,0:T(8,128)(2,1)S(1)}, bf16[4,8,2048]{2,1,0:T(8,128)(2,1)}, u32[]{:S(2)}) copy-start(bf16[4,8,2048]{2,1,0:T(8,128)(2,1)} %param.9) | copy-start | bytes 393220
  86.3 205.2 %all-gather.6.cloned.1.call-start = ((), (), s32[]{:S(2)}) async-start(), calls=%async_computation.4 | async-start | bytes 4325376 | tf_op jit(solution)/shard_map/all_gather | solution.py:170
  231.0 214.2 %reduce-scatter.5.cloned.1.call-start = ((), (), s32[]{:S(2)}) async-start(), calls=%async_computation.5 | async-start | bytes 4325376 | tf_op jit(solution)/shard_map/reduce_scatter | solution.py:176
Sparse Core Ops, SparseCore 0:
  10.4 64.8 all-gather.3
  86.4 142.5 reduce-scatter.2
  232.1 59.3 all-gather.5
  302.6 142.5 reduce-scatter.4

commit v2 on v1

v2 whole, which is shorter than its diff:
```python
import jax
import jax.numpy as jnp
from jax import lax
from jax.sharding import PartitionSpec as P

CAP = 2


epsilon = 1e-06


def spread(block, axis, owner):
    block = jnp.where(lax.axis_index(axis) == owner, block, jnp.zeros_like(block))
    return lax.psum(block, axis)


def slot_plan(target, groups, capacity):
    count = target.shape[0]
    earlier = jnp.arange(count)[None, :] < jnp.arange(count)[:, None]
    same = target[:, None] == target[None, :]
    within = jnp.sum(jnp.logical_and(same, earlier).astype(jnp.int32), axis=1)
    slot = target * capacity + within
    return (jnp.arange(groups * capacity)[:, None] == slot[None, :]).astype(jnp.bfloat16)


def into_slots(taken, items):
    flat = items.reshape(items.shape[0], -1)
    placed = jnp.dot(taken, flat, preferred_element_type=jnp.float32).astype(items.dtype)
    return placed.reshape((-1,) + items.shape[1:])


def from_slots(taken, slots):
    return into_slots(taken.T, slots)


def swap(value, distance):
    size = lax.axis_size("roll")
    return lax.ppermute(value, "roll", [(place, place ^ distance) for place in range(size)])


def fetch_layers(gate_up, down, owners, layer_count):
    me = lax.axis_index("roll")
    upper = lax.rem(me, 2) == 1
    kept, given = [], []
    for master in (gate_up[0, 0], down[0, 0]):
        middle = master.shape[0] // 2
        low, high = master[:middle].astype(jnp.bfloat16), master[middle:].astype(jnp.bfloat16)
        kept.append(jnp.where(upper, high, low))
        given.append(jnp.where(upper, low, high))
    got = [swap(half, 1) for half in given]
    layers, before = [], None
    for layer_index in range(layer_count):
        owner = owners[layer_index]
        halves = [
            jnp.where(owner == me, mine, jnp.where(owner == me ^ 1, theirs, jnp.zeros_like(mine)))
            for mine, theirs in zip(kept, got)
        ]
        if before is not None:
            halves, _ = lax.optimization_barrier((halves, before))
        distance = 2
        while distance < lax.axis_size("roll"):
            before = [swap(half, distance) for half in halves]
            halves = [half + other for half, other in zip(halves, before)]
            distance *= 2
        weights = []
        for half in halves:
            other = swap(half, 1)
            weights.append(
                jnp.concatenate([jnp.where(upper, other, half), jnp.where(upper, half, other)], axis=0)
            )
        layers.append(tuple(weights))
    return layers


def send_rows_out(current, lengths, taken):
    got_rows = lax.all_to_all(into_slots(taken, current), "roll", split_axis=0, concat_axis=0, tiled=True)
    send_lengths = jnp.sum(jnp.where(taken > 0, lengths[None, :], 0), axis=1)
    got_lengths = lax.all_to_all(send_lengths[:, None], "roll", split_axis=0, concat_axis=0, tiled=True)
    return (got_rows, got_lengths[:, 0])


def send_home(combined, taken):
    home_rows = lax.all_to_all(combined, "roll", split_axis=0, concat_axis=0, tiled=True)
    return from_slots(taken, home_rows)


def process_rows(held, held_lengths, weights, layer_gain, route_column, weight_column):
    tp_size = lax.axis_size("tp")
    row_tokens = held.shape[1]
    model_width = held.shape[2]
    received = held.reshape(-1, model_width)
    token_count = received.shape[0]
    present = (jnp.arange(row_tokens)[None, :] < held_lengths[:, None]).reshape(-1)
    widened = received.astype(jnp.float32)
    normed = (
        widened
        * lax.rsqrt(jnp.mean(widened * widened, axis=1, keepdims=True) + epsilon)
        * layer_gain[None, :]
    ).astype(jnp.bfloat16)
    expert_slots = 5 * token_count // (4 * tp_size)
    taken = slot_plan(route_column, tp_size, expert_slots)
    send_tokens = into_slots(taken, normed).reshape(tp_size, expert_slots, model_width)
    gate_up_w, down_w = weights
    hidden_width = down_w.shape[0]
    arrived = lax.all_to_all(send_tokens, "tp", split_axis=0, concat_axis=0, tiled=True)
    flattened = arrived.reshape(-1, model_width)
    projected = jnp.dot(flattened, gate_up_w, preferred_element_type=jnp.float32)
    hidden = (jax.nn.silu(projected[:, :hidden_width]) * projected[:, hidden_width:]).astype(
        jnp.bfloat16
    )
    produced = jnp.dot(hidden, down_w, preferred_element_type=jnp.float32).astype(jnp.bfloat16)
    returned = lax.all_to_all(
        produced.reshape(arrived.shape), "tp", split_axis=0, concat_axis=0, tiled=True
    )
    answer = from_slots(taken, returned.reshape(-1, model_width))
    combined = (
        widened
        + (present.astype(jnp.float32) * weight_column)[:, None] * answer.astype(jnp.float32)
    ).astype(jnp.bfloat16)
    return combined.reshape(held.shape)


def per_device(tokens, lengths, plan, owners, gate_up, down, norm_gain, routing, route_weight):
    layer_count = plan.shape[0]
    roll_size = lax.axis_size("roll")
    plans = [
        slot_plan(plan[layer_index, :, 0], roll_size, CAP) for layer_index in range(layer_count)
    ]
    weights = fetch_layers(gate_up, down, owners, layer_count)
    current = tokens
    for layer_index in range(layer_count):
        held, held_lengths = send_rows_out(current, lengths, plans[layer_index])
        combined = process_rows(
            held,
            held_lengths,
            weights[layer_index],
            norm_gain[layer_index],
            routing[layer_index, :, 0],
            route_weight[layer_index],
        )
        current = send_home(combined, plans[layer_index])
    return current


def solution(mesh):
    in_specs = (
        P(("roll", "tp"), None, None),
        P(("roll", "tp")),
        P(None, ("roll", "tp"), None),
        P(),
        P("roll", "tp", None, None),
        P("roll", "tp", None, None),
        P(),
        P(None, ("roll", "tp"), None),
        P(None, ("roll", "tp")),
    )
    out_specs = P(("roll", "tp"), None, None)
    return jax.shard_map(
        per_device, mesh=mesh, in_specs=in_specs, out_specs=out_specs, check_vma=False
    )
```

time: 454 us -> 224 us (0.49)
  waiting for transfers between devices: 360 us -> 112 us
  starting transfers between devices: 0.13 us -> 36.3 us
  other arithmetic: 8.71 us -> 27.5 us
  matrix products: 21.9 us -> 5.08 us
  blocking collectives: 42.5 us -> 26.5 us
  between operations: 14.5 us -> 2.87 us
  local copies, waits for them, and re-layouts: 5.64 us -> 13 us
    reduce_scatter x2 -> x0, waiting for transfers between devices: 284 us -> none  [per_device_gathered(): lax.psum_scatter(produced, ('roll', 'tp'), scatter_dimension=0, tiled=True)]
    all_gather x2 -> x0, waiting for transfers between devices: 75.4 us -> none  [per_device_gathered(): arrived = lax.all_gather(normed, ('roll', 'tp'), tiled=True)]
    all_to_all x0 -> x8, waiting for transfers between devices: none -> 59.8 us  [the longest x2 25.2 us: process_rows(): lax.all_to_all(send_tokens, 'tp', split_axis=0, concat_axis=0, tiled=True)]
    ppermute x0 -> x10, waiting for transfers between devices: none -> 51.9 us  [swap(): lax.ppermute(value, 'roll', [(place, place ^ distance) for place in range...]
    unnamed x1 -> x0, blocking collectives: 42.5 us -> none
    all_to_all x0 -> x8, starting transfers between devices: none -> 30.6 us  [the longest x2 9.72 us: process_rows(): lax.all_to_all(send_tokens, 'tp', split_axis=0, concat_axis=0, tiled=True)]
    all_to_all x0 -> x2, blocking collectives: none -> 26.5 us  [the longest x1 18 us: process_rows(): lax.all_to_all(produced.reshape(arrived.shape), 'tp', split_axis=0, conca...]
    dot_general x4 -> x11, matrix products: 21.9 us -> 5.08 us  [the longest x7 2.93 us: into_slots(): jnp.dot(taken, flat, preferred_element_type=jnp.float32).astype(items.dtype)]
  transfers between devices with their start and end apart: 4 -> 18, of which waited for: 4 -> 8; matrix products, arithmetic and copies ran while one was open for 1% -> 15% of each run, Pallas kernels for 0% -> 0%
where the time goes in v2:
time: 224 us; the launch traced here: 223 us
  waiting for transfers between devices  112 us (50%)
  starting transfers between devices  36.3 us (16%)
  other arithmetic  27.5 us (12%)
  blocking collectives  26.5 us (12%)
  local copies, waits for them, and re-layouts  13 us (6%)
  matrix products  5.08 us (2%)
  between operations  2.87 us (1%)
    ppermute x10, waiting for transfers between devices, swap(): lax.ppermute(value, 'roll', [(place, place ^ distance) for place in range...  51.9 us
    all_to_all x2, waiting for transfers between devices, process_rows(): lax.all_to_all(send_tokens, 'tp', split_axis=0, concat_axis=0, tiled=True)  25.2 us
    all_to_all x1, blocking collectives, process_rows(): lax.all_to_all(produced.reshape(arrived.shape), 'tp', split_axis=0, conca...  18 us
    all_to_all x1, waiting for transfers between devices, send_home(): lax.all_to_all(combined, 'roll', split_axis=0, concat_axis=0, tiled=True)  17.3 us
    all_to_all x1, waiting for transfers between devices, process_rows(): lax.all_to_all(produced.reshape(arrived.shape), 'tp', split_axis=0, conca...  13.5 us
    all_to_all x2, starting transfers between devices, process_rows(): lax.all_to_all(send_tokens, 'tp', split_axis=0, concat_axis=0, tiled=True)  9.72 us
    all_to_all x1, blocking collectives, send_home(): lax.all_to_all(combined, 'roll', split_axis=0, concat_axis=0, tiled=True)  8.42 us
    all_to_all x2, starting transfers between devices, send_rows_out(): lax.all_to_all(into_slots(taken, current), 'roll', split_axis=0, concat_a...  7.27 us
  transfers between devices with their start and end apart: 18, of which 8 were waited for; matrix products, arithmetic and copies ran while one was open for 15% of the time, Pallas kernels for 0%

profile of v2, /device:TPU:0, one launch (start us, length us, event | category | flops | bytes accessed | tf_op | source)
XLA Modules:
  0.0 222.8 jit_solution(8726954247515005727)
XLA Ops:
  0.0 3.1 %convert.10 = bf16[1,1,2048,768]{3,2,1,0:T(8,128)(2,1)S(1)} convert(f32[1,1,2048,768]{3,2,1,0:T(8,128)} %param.13) | non-fusion elementwise | flops 1572864 | bytes 9437184 | tf_op jit(solution)/shard_map/convert.5
  10.0 3.9 %all-to-all-start = ((bf16[8,8,2048]{2,1,0:T(8,128)(2,1)}), bf16[8,8,2048]{2,1,0:T(8,128)(2,1)S(1)}, u32[]{:S(2)}, u32[]{:S(2)}) async-start(bf16[8,8,2048]{2,1,0:T(8,128)(2,1)} %copy.22), calls=%async_computation | async-start | bytes 524288 | tf_op jit(solution)/shard_map/all_to_all | solution.py:76
  17.0 3.5 %bitcast_select_fusion.1 = (bf16[1024,768]{1,0:T(8,128)(2,1)}, bf16[1024,768]{1,0:T(8,128)(2,1)}) fusion(bf16[1024,768]{1,0:T(8,128)(2,1)} %collective-permute-done, pred[]{:T(512)S(6)} %eq.143, pred[]{:T(512)S(6)} %eq.142, bf16[1,1,2048,768]{3,2,1,0:T(8,128)(2,1)S(1)} %convert.10, pred[]{:T(512)S(6)} %eq.141, pred[]{:T(512)S(6)} %eq.151, pred[]{:T(512)S(6)} %eq.150), kind=kLoop, calls=%fused_computation.35 | loop fusion | flops 3932160 | bytes 7864325 | tf_op jit(solution)/shard_map/jit(_where)/select_n | solution.py:55
  20.5 2.0 collective-permute-start.1
  22.5 2.2 bitcast_select_fusion.3
  25.7 32.4 %collective-permute-done.1 = bf16[1024,768]{1,0:T(8,128)(2,1)} collective-permute-done((bf16[1024,768]{1,0:T(8,128)(2,1)}, bf16[1024,768]{1,0:T(8,128)(2,1)}, u32[]{:S(2)}, u32[]{:S(2)}) %collective-permute-start.1) | collective-permute-done | bytes 1572896 | tf_op jit(solution)/shard_map/ppermute | solution.py:38
  58.0 2.3 %add.75 = bf16[1024,768]{1,0:T(8,128)(2,1)S(1)} add(bf16[1024,768]{1,0:T(8,128)(2,1)} %get-tuple-element.11, bf16[1024,768]{1,0:T(8,128)(2,1)} %collective-permute-done.1) | non-fusion elementwise | flops 786432 | bytes 4718592 | tf_op jit(solution)/shard_map/add | solution.py:63
  60.4 3.3 %all-to-all-start.6 = ((s32[4,2,1]{1,2,0:T(1,128)}), s32[4,2,1]{1,2,0:T(1,128)S(1)}, u32[]{:S(2)}, u32[]{:S(2)}) async-start(s32[4,2,1]{1,2,0:T(1,128)} %bitcast.16), calls=%async_computation.6 | async-start | bytes 4096 | tf_op jit(solution)/shard_map/all_to_all | solution.py:78
  64.1 10.5 %collective-permute-done.4 = bf16[192,2048]{1,0:T(8,128)(2,1)S(1)} collective-permute-done((bf16[192,2048]{1,0:T(8,128)(2,1)S(1)}, bf16[192,2048]{1,0:T(8,128)(2,1)S(1)}, u32[]{:S(2)}, u32[]{:S(2)}) %collective-permute-start.4) | collective-permute-done | bytes 786464 | tf_op jit(solution)/shard_map/ppermute | solution.py:38
  77.0 6.1 %all-to-all-start.2 = ((bf16[8,10,2048]{2,1,0:T(8,128)(2,1)}), bf16[8,10,2048]{2,1,0:T(8,128)(2,1)S(1)}, u32[]{:S(2)}, u32[]{:S(2)}) async-start(bf16[8,10,2048]{2,1,0:T(8,128)(2,1)} %reshape.191), calls=%async_computation.2 | async-start | bytes 1048576 | tf_op jit(solution)/shard_map/all_to_all | solution.py:105
  85.0 13.3 %all-to-all-done.2 = bf16[8,10,2048]{2,1,0:T(8,128)(2,1)S(1)} async-done(((bf16[8,10,2048]{2,1,0:T(8,128)(2,1)}), bf16[8,10,2048]{2,1,0:T(8,128)(2,1)S(1)}, u32[]{:S(2)}, u32[]{:S(2)}) %all-to-all-start.2) | async-done | bytes 327712 | tf_op jit(solution)/shard_map/all_to_all | solution.py:105
  98.3 3.2 %all-to-all-start.1 = ((s32[4,2,1]{1,2,0:T(1,128)}), s32[4,2,1]{1,2,0:T(1,128)S(1)}, u32[]{:S(2)}, u32[]{:S(2)}) async-start(s32[4,2,1]{1,2,0:T(1,128)} %bitcast.4), calls=%async_computation.1 | async-start | bytes 4096 | tf_op jit(solution)/shard_map/all_to_all | solution.py:78
  109.8 3.7 %all-to-all-start.3 = ((bf16[8,10,2048]{2,1,0:T(8,128)(2,1)}), bf16[8,10,2048]{2,1,0:T(8,128)(2,1)S(1)}, u32[]{:S(2)}, u32[]{:S(2)}) async-start(bf16[8,10,2048]{2,1,0:T(8,128)(2,1)} %reshape.193), calls=%async_computation.3 | async-start | bytes 1048576 | tf_op jit(solution)/shard_map/all_to_all | solution.py:112
  114.6 13.5 %all-to-all-done.3 = bf16[8,10,2048]{2,1,0:T(8,128)(2,1)S(1)} async-done(((bf16[8,10,2048]{2,1,0:T(8,128)(2,1)}), bf16[8,10,2048]{2,1,0:T(8,128)(2,1)S(1)}, u32[]{:S(2)}, u32[]{:S(2)}) %all-to-all-start.3) | async-done | bytes 327712 | tf_op jit(solution)/shard_map/all_to_all | solution.py:112
  129.2 3.4 %all-to-all-start.4 = ((bf16[8,8,2048]{2,1,0:T(8,128)(2,1)}), bf16[8,8,2048]{2,1,0:T(8,128)(2,1)S(1)}, u32[]{:S(2)}, u32[]{:S(2)}) async-start(bf16[8,8,2048]{2,1,0:T(8,128)(2,1)} %fusion.16), calls=%async_computation.4 | async-start | bytes 524288 | tf_op jit(solution)/shard_map/all_to_all | solution.py:83
  132.6 9.0 %collective-permute-done.6 = bf16[1024,768]{1,0:T(8,128)(2,1)} collective-permute-done((bf16[1024,768]{1,0:T(8,128)(2,1)S(1)}, bf16[1024,768]{1,0:T(8,128)(2,1)}, u32[]{:S(2)}, u32[]{:S(2)}) %collective-permute-start.6) | collective-permute-done | bytes 1572896 | tf_op jit(solution)/shard_map/ppermute | solution.py:38
  143.4 17.3 %all-to-all-done.4 = bf16[8,8,2048]{2,1,0:T(8,128)(2,1)S(1)} async-done(((bf16[8,8,2048]{2,1,0:T(8,128)(2,1)}), bf16[8,8,2048]{2,1,0:T(8,128)(2,1)S(1)}, u32[]{:S(2)}, u32[]{:S(2)}) %all-to-all-start.4) | async-done | bytes 262176 | tf_op jit(solution)/shard_map/all_to_all | solution.py:83
  162.1 3.4 %all-to-all-start.5 = ((bf16[8,8,2048]{2,1,0:T(8,128)(2,1)}), bf16[8,8,2048]{2,1,0:T(8,128)(2,1)S(1)}, u32[]{:S(2)}, u32[]{:S(2)}) async-start(bf16[8,8,2048]{2,1,0:T(8,128)(2,1)} %copy.26), calls=%async_computation.5 | async-start | bytes 524288 | tf_op jit(solution)/shard_map/all_to_all | solution.py:76
  167.7 3.8 %all-to-all-done.5 = bf16[8,8,2048]{2,1,0:T(8,128)(2,1)S(1)} async-done(((bf16[8,8,2048]{2,1,0:T(8,128)(2,1)}), bf16[8,8,2048]{2,1,0:T(8,128)(2,1)S(1)}, u32[]{:S(2)}, u32[]{:S(2)}) %all-to-all-start.5) | async-done | bytes 262176 | tf_op jit(solution)/shard_map/all_to_all | solution.py:76
  173.1 3.6 %all-to-all-start.7 = ((bf16[8,10,2048]{2,1,0:T(8,128)(2,1)}), bf16[8,10,2048]{2,1,0:T(8,128)(2,1)S(1)}, u32[]{:S(2)}, u32[]{:S(2)}) async-start(bf16[8,10,2048]{2,1,0:T(8,128)(2,1)} %reshape.198), calls=%async_computation.7 | async-start | bytes 1048576 | tf_op jit(solution)/shard_map/all_to_all | solution.py:105
  176.8 2.4 %broadcast_select_fusion.7 = (bf16[192,2048]{1,0:T(8,128)(2,1)}, bf16[192,2048]{1,0:T(8,128)(2,1)}) fusion(bf16[192,2048]{1,0:T(8,128)(2,1)} %collective-permute-done.9, bf16[192,2048]{1,0:T(8,128)(2,1)S(1)} %add.83, pred[]{:T(512)S(6)} %eq.141), kind=kLoop, calls=%fused_computation.47 | loop fusion | flops 786432 | bytes 3145729 | tf_op jit(solution)/shard_map/jit(_where)/select_n | solution.py:69
  179.2 11.9 %all-to-all-done.7 = bf16[8,10,2048]{2,1,0:T(8,128)(2,1)S(1)} async-done(((bf16[8,10,2048]{2,1,0:T(8,128)(2,1)}), bf16[8,10,2048]{2,1,0:T(8,128)(2,1)S(1)}, u32[]{:S(2)}, u32[]{:S(2)}) %all-to-all-start.7) | async-done | bytes 327712 | tf_op jit(solution)/shard_map/all_to_all | solution.py:105
  194.8 18.0 %all_to_all.58 = bf16[8,10,2048]{2,1,0:T(8,128)(2,1)S(1)} all-to-all(bf16[8,10,2048]{2,1,0:T(8,128)(2,1)S(1)} %reshape.200), channel_id=1, replica_groups=mesh['roll'=4,'tp'=8] {'tp'}, dimensions={0} | all-to-all | bytes 655360 | tf_op jit(solution)/shard_map/all_to_all | solution.py:112
  213.2 8.4 %all_to_all.59 = bf16[8,8,2048]{2,1,0:T(8,128)(2,1)S(1)} all-to-all(bf16[8,8,2048]{2,1,0:T(8,128)(2,1)S(1)} %fusion.17), channel_id=1, replica_groups=mesh['roll'=4,'tp'=8] {'roll'}, dimensions={0} | all-to-all | bytes 524288 | tf_op jit(solution)/shard_map/all_to_all | solution.py:83
  (112 shorter events, 35.9 us)
Async XLA Ops:
  4.5 12.5 %collective-permute-start = (bf16[1024,768]{1,0:T(8,128)(2,1)}, bf16[1024,768]{1,0:T(8,128)(2,1)}, u32[]{:S(2)}, u32[]{:S(2)}) collective-permute-start(bf16[1024,768]{1,0:T(8,128)(2,1)} %select_bitcast_fusion), channel_id=1, source_target_pairs={{0,8},{8,0},{16,24},{24,16},{1,9},{9,1},{17,25},{25,17},{2,10},{10... | collective-permute-start | bytes 4718600 | tf_op jit(solution)/shard_map/ppermute | solution.py:38
  6.9 6.9 %copy-start.11 = (s32[4]{0:T(128)S(1)}, s32[4]{0:T(128)}, u32[]{:S(2)}) copy-start(s32[4]{0:T(128)} %param.12) | copy-start | bytes 52
  7.9 14.6 %collective-permute-start.3 = (bf16[192,2048]{1,0:T(8,128)(2,1)}, bf16[192,2048]{1,0:T(8,128)(2,1)}, u32[]{:S(2)}, u32[]{:S(2)}) collective-permute-start(bf16[192,2048]{1,0:T(8,128)(2,1)} %select_bitcast_fusion.1), channel_id=1, source_target_pairs={{0,8},{8,0},{16,24},{24,16},{1,9},{9,1},{17,25},{25,17},{2,10},{10... | collective-permute-start | bytes 2359304 | tf_op jit(solution)/shard_map/ppermute | solution.py:38
  10.0 50.4 %all-to-all-start = ((bf16[8,8,2048]{2,1,0:T(8,128)(2,1)}), bf16[8,8,2048]{2,1,0:T(8,128)(2,1)S(1)}, u32[]{:S(2)}, u32[]{:S(2)}) async-start(bf16[8,8,2048]{2,1,0:T(8,128)(2,1)} %copy.22), calls=%async_computation | async-start | bytes 524288 | tf_op jit(solution)/shard_map/all_to_all | solution.py:76
  17.0 5.5 %copy-start.10 = (s32[2,64,1]{1,2,0:T(1,128)S(1)}, s32[2,64,1]{1,2,0:T(1,128)}, u32[]{:S(2)}) copy-start(s32[2,64,1]{1,2,0:T(1,128)} %param.16) | copy-start | bytes 1540
  17.0 5.5 %copy-start.8 = (f32[2,2048]{1,0:T(2,128)S(1)}, f32[2,2048]{1,0:T(2,128)}, u32[]{:S(2)}) copy-start(f32[2,2048]{1,0:T(2,128)} %param.15) | copy-start | bytes 49156
  17.0 5.6 %copy-start.1 = (bf16[1,1,384,2048]{3,2,1,0:T(8,128)(2,1)S(1)}, bf16[1,1,384,2048]{3,2,1,0:T(8,128)(2,1)}, u32[]{:S(2)}) copy-start(bf16[1,1,384,2048]{3,2,1,0:T(8,128)(2,1)} %copy-done) | copy-start | bytes 4718596
  20.5 37.6 %collective-permute-start.1 = (bf16[1024,768]{1,0:T(8,128)(2,1)}, bf16[1024,768]{1,0:T(8,128)(2,1)}, u32[]{:S(2)}, u32[]{:S(2)}) collective-permute-start(bf16[1024,768]{1,0:T(8,128)(2,1)} %get-tuple-element.11), channel_id=1, source_target_pairs={{0,16},{8,24},{16,0},{24,8},{1,17},{9,25},{17,1},{25,9},{2,18},{10... | collective-permute-start | bytes 4718600 | tf_op jit(solution)/shard_map/ppermute | solution.py:38
  24.7 49.9 %collective-permute-start.4 = (bf16[192,2048]{1,0:T(8,128)(2,1)S(1)}, bf16[192,2048]{1,0:T(8,128)(2,1)S(1)}, u32[]{:S(2)}, u32[]{:S(2)}) collective-permute-start(bf16[192,2048]{1,0:T(8,128)(2,1)S(1)} %get-tuple-element.17), channel_id=1, source_target_pairs={{0,16},{8,24},{16,0},{24,8},{1,17},{9,25},{17,1},{25,9},{2,18},{10... | collective-permute-start | bytes 2359304 | tf_op jit(solution)/shard_map/ppermute | solution.py:38
  60.3 45.9 %collective-permute-start.2 = (bf16[1024,768]{1,0:T(8,128)(2,1)S(1)}, bf16[1024,768]{1,0:T(8,128)(2,1)}, u32[]{:S(2)}, u32[]{:S(2)}) collective-permute-start(bf16[1024,768]{1,0:T(8,128)(2,1)S(1)} %add.75), channel_id=1, source_target_pairs={{0,8},{8,0},{16,24},{24,16},{1,9},{9,1},{17,25},{25,17},{2,10},{10... | collective-permute-start | bytes 4718600 | tf_op jit(solution)/shard_map/ppermute | solution.py:38
  60.4 16.6 %all-to-all-start.6 = ((s32[4,2,1]{1,2,0:T(1,128)}), s32[4,2,1]{1,2,0:T(1,128)S(1)}, u32[]{:S(2)}, u32[]{:S(2)}) async-start(s32[4,2,1]{1,2,0:T(1,128)} %bitcast.16), calls=%async_computation.6 | async-start | bytes 4096 | tf_op jit(solution)/shard_map/all_to_all | solution.py:78
  75.8 26.6 %collective-permute-start.5 = (bf16[192,2048]{1,0:T(8,128)(2,1)}, bf16[192,2048]{1,0:T(8,128)(2,1)}, u32[]{:S(2)}, u32[]{:S(2)}) collective-permute-start(bf16[192,2048]{1,0:T(8,128)(2,1)} %add.77), channel_id=1, source_target_pairs={{0,8},{8,0},{16,24},{24,16},{1,9},{9,1},{17,25},{25,17},{2,10},{10... | collective-permute-start | bytes 2359304 | tf_op jit(solution)/shard_map/ppermute | solution.py:38
  77.0 21.2 %all-to-all-start.2 = ((bf16[8,10,2048]{2,1,0:T(8,128)(2,1)}), bf16[8,10,2048]{2,1,0:T(8,128)(2,1)S(1)}, u32[]{:S(2)}, u32[]{:S(2)}) async-start(bf16[8,10,2048]{2,1,0:T(8,128)(2,1)} %reshape.191), calls=%async_computation.2 | async-start | bytes 1048576 | tf_op jit(solution)/shard_map/all_to_all | solution.py:105
  98.3 11.6 %all-to-all-start.1 = ((s32[4,2,1]{1,2,0:T(1,128)}), s32[4,2,1]{1,2,0:T(1,128)S(1)}, u32[]{:S(2)}, u32[]{:S(2)}) async-start(s32[4,2,1]{1,2,0:T(1,128)} %bitcast.4), calls=%async_computation.1 | async-start | bytes 4096 | tf_op jit(solution)/shard_map/all_to_all | solution.py:78
  104.2 3.6 %copy-start.6 = (bf16[80,2048]{1,0:T(8,128)(2,1)S(1)}, bf16[80,2048]{1,0:T(8,128)(2,1)}, u32[]{:S(2)}) copy-start(bf16[80,2048]{1,0:T(8,128)(2,1)} %reshape.192) | copy-start | bytes 983044
  104.2 37.3 %collective-permute-start.6 = (bf16[1024,768]{1,0:T(8,128)(2,1)S(1)}, bf16[1024,768]{1,0:T(8,128)(2,1)}, u32[]{:S(2)}, u32[]{:S(2)}) collective-permute-start(bf16[1024,768]{1,0:T(8,128)(2,1)S(1)} %copy-done.2), channel_id=1, source_target_pairs={{0,16},{8,24},{16,0},{24,8},{1,17},{9,25},{17,1},{25,9},{2,18},{10... | collective-permute-start | bytes 4718600 | tf_op jit(solution)/shard_map/ppermute | solution.py:38
  108.9 5.7 %copy-start.12 = (f32[2,64]{1,0:T(2,128)S(1)}, f32[2,64]{1,0:T(2,128)}, u32[]{:S(2)}) copy-start(f32[2,64]{1,0:T(2,128)} %param.17) | copy-start | bytes 1540
  109.8 18.2 %all-to-all-start.3 = ((bf16[8,10,2048]{2,1,0:T(8,128)(2,1)}), bf16[8,10,2048]{2,1,0:T(8,128)(2,1)S(1)}, u32[]{:S(2)}, u32[]{:S(2)}) async-start(bf16[8,10,2048]{2,1,0:T(8,128)(2,1)} %reshape.193), calls=%async_computation.3 | async-start | bytes 1048576 | tf_op jit(solution)/shard_map/all_to_all | solution.py:112
  114.5 51.0 %collective-permute-start.8 = (bf16[192,2048]{1,0:T(8,128)(2,1)}, bf16[192,2048]{1,0:T(8,128)(2,1)}, u32[]{:S(2)}, u32[]{:S(2)}) collective-permute-start(bf16[192,2048]{1,0:T(8,128)(2,1)} %get-tuple-element.8), channel_id=1, source_target_pairs={{0,16},{8,24},{16,0},{24,8},{1,17},{9,25},{17,1},{25,9},{2,18},{10... | collective-permute-start | bytes 2359304 | tf_op jit(solution)/shard_map/ppermute | solution.py:38
  129.2 31.5 %all-to-all-start.4 = ((bf16[8,8,2048]{2,1,0:T(8,128)(2,1)}), bf16[8,8,2048]{2,1,0:T(8,128)(2,1)S(1)}, u32[]{:S(2)}, u32[]{:S(2)}) async-start(bf16[8,8,2048]{2,1,0:T(8,128)(2,1)} %fusion.16), calls=%async_computation.4 | async-start | bytes 524288 | tf_op jit(solution)/shard_map/all_to_all | solution.py:83
  143.3 47.9 %collective-permute-start.7 = (bf16[1024,768]{1,0:T(8,128)(2,1)S(1)}, bf16[1024,768]{1,0:T(8,128)(2,1)}, u32[]{:S(2)}, u32[]{:S(2)}) collective-permute-start(bf16[1024,768]{1,0:T(8,128)(2,1)S(1)} %add.81), channel_id=1, source_target_pairs={{0,8},{8,0},{16,24},{24,16},{1,9},{9,1},{17,25},{25,17},{2,10},{10... | collective-permute-start | bytes 4718600 | tf_op jit(solution)/shard_map/ppermute | solution.py:38
  162.1 9.4 %all-to-all-start.5 = ((bf16[8,8,2048]{2,1,0:T(8,128)(2,1)}), bf16[8,8,2048]{2,1,0:T(8,128)(2,1)S(1)}, u32[]{:S(2)}, u32[]{:S(2)}) async-start(bf16[8,8,2048]{2,1,0:T(8,128)(2,1)} %copy.26), calls=%async_computation.5 | async-start | bytes 524288 | tf_op jit(solution)/shard_map/all_to_all | solution.py:76
  167.2 9.6 %collective-permute-start.9 = (bf16[192,2048]{1,0:T(8,128)(2,1)S(1)}, bf16[192,2048]{1,0:T(8,128)(2,1)}, u32[]{:S(2)}, u32[]{:S(2)}) collective-permute-start(bf16[192,2048]{1,0:T(8,128)(2,1)S(1)} %add.83), channel_id=1, source_target_pairs={{0,8},{8,0},{16,24},{24,16},{1,9},{9,1},{17,25},{25,17},{2,10},{10... | collective-permute-start | bytes 2359304 | tf_op jit(solution)/shard_map/ppermute | solution.py:38
  173.1 18.0 %all-to-all-start.7 = ((bf16[8,10,2048]{2,1,0:T(8,128)(2,1)}), bf16[8,10,2048]{2,1,0:T(8,128)(2,1)S(1)}, u32[]{:S(2)}, u32[]{:S(2)}) async-start(bf16[8,10,2048]{2,1,0:T(8,128)(2,1)} %reshape.198), calls=%async_computation.7 | async-start | bytes 1048576 | tf_op jit(solution)/shard_map/all_to_all | solution.py:105
  (8 other events, 13.2 us)

commit v3 on v2

v3 whole, which is shorter than its diff:
```python
import jax
import jax.numpy as jnp
from jax import lax
from jax.sharding import PartitionSpec as P

CAP = 2


epsilon = 1e-06


def spread(block, axis, owner):
    block = jnp.where(lax.axis_index(axis) == owner, block, jnp.zeros_like(block))
    return lax.psum(block, axis)


def slot_plan(target, groups, capacity):
    count = target.shape[0]
    earlier = jnp.arange(count)[None, :] < jnp.arange(count)[:, None]
    same = target[:, None] == target[None, :]
    within = jnp.sum(jnp.logical_and(same, earlier).astype(jnp.int32), axis=1)
    slot = target * capacity + within
    return (jnp.arange(groups * capacity)[:, None] == slot[None, :]).astype(jnp.bfloat16)


def into_slots(taken, items):
    flat = items.reshape(items.shape[0], -1)
    placed = jnp.dot(taken, flat, preferred_element_type=jnp.float32).astype(items.dtype)
    return placed.reshape((-1,) + items.shape[1:])


def from_slots(taken, slots):
    return into_slots(taken.T, slots)


def swap(value, distance):
    size = lax.axis_size("roll")
    return lax.ppermute(value, "roll", [(place, place ^ distance) for place in range(size)])


def share_halves(gate_up, down):
    upper = lax.rem(lax.axis_index("roll"), 2) == 1
    kept, given = [], []
    for master in (gate_up[0, 0], down[0, 0]):
        middle = master.shape[0] // 2
        low, high = master[:middle].astype(jnp.bfloat16), master[middle:].astype(jnp.bfloat16)
        kept.append(jnp.where(upper, high, low))
        given.append(jnp.where(upper, low, high))
    return kept, [swap(half, 1) for half in given]


def cross(kept, got, owner, before):
    me = lax.axis_index("roll")
    halves = [
        jnp.where(owner == me, mine, jnp.where(owner == me ^ 1, theirs, jnp.zeros_like(mine)))
        for mine, theirs in zip(kept, got)
    ]
    if before is not None:
        halves, _ = lax.optimization_barrier((halves, before))
    others = [jnp.zeros_like(half) for half in halves]
    distance = 2
    while distance < lax.axis_size("roll"):
        halves = [half + other for half, other in zip(halves, others)] if distance > 2 else halves
        others = [swap(half, distance) for half in halves]
        distance *= 2
    return halves, others


def complete(halves, others):
    upper = lax.rem(lax.axis_index("roll"), 2) == 1
    weights = []
    for half, other in zip(halves, others):
        half = half + other
        other = swap(half, 1)
        weights.append(
            jnp.concatenate([jnp.where(upper, other, half), jnp.where(upper, half, other)], axis=0)
        )
    return weights


def share_plan(plan, lengths, roll_size):
    layer_count, rows_dev = plan.shape[0], plan.shape[1]
    packed = jnp.concatenate([plan[:, :, 0].reshape(-1), lengths])
    sent = jnp.broadcast_to(packed[None, :], (roll_size, packed.shape[0]))
    got = lax.all_to_all(sent, "roll", split_axis=0, concat_axis=0, tiled=True)
    return got[:, :-rows_dev].reshape(roll_size, layer_count, rows_dev), got[:, -rows_dev:]


def held_lengths(owner, row_lengths):
    me, count = lax.axis_index("roll"), owner.shape[1]
    earlier = jnp.arange(count)[None, :] < jnp.arange(count)[:, None]
    same = owner[:, :, None] == owner[:, None, :]
    within = jnp.sum(jnp.logical_and(same, earlier[None]).astype(jnp.int32), axis=2)
    here = jnp.logical_and(
        (owner == me)[:, None, :], within[:, None, :] == jnp.arange(CAP)[None, :, None]
    )
    return jnp.sum(jnp.where(here, row_lengths[:, None, :], 0), axis=2).reshape(-1)


def forward_plan(previous, owner, roll_size):
    me = lax.axis_index("roll")
    homes = jnp.arange(roll_size)
    turned = lax.rem(owner - homes[:, None] + roll_size, roll_size)
    turn = jnp.max(
        jnp.where(previous[:, :, None] == homes[None, None, :], turned[:, :, None], -1), axis=(0, 1)
    )
    mine = jnp.max(jnp.where(homes == me, turn, -1))
    to_send = jnp.logical_and(mine >= 0, homes[:, None] == lax.rem(homes[None, :] + mine, roll_size))
    to_keep = jnp.logical_and(turn[None, :] >= 0, lax.rem(homes[:, None] + turn[None, :], roll_size) == me)
    return to_send.astype(jnp.bfloat16), to_keep.astype(jnp.bfloat16)


def forward_rows(combined, moves, roll_size):
    chunks = into_slots(moves[0], combined.reshape((roll_size, CAP) + combined.shape[1:]))
    came = lax.all_to_all(chunks, "roll", split_axis=0, concat_axis=0, tiled=True)
    return into_slots(moves[1], came).reshape(combined.shape)


def send_home(combined, taken):
    home_rows = lax.all_to_all(combined, "roll", split_axis=0, concat_axis=0, tiled=True)
    return from_slots(taken, home_rows)


def process_rows(held, slot_lengths, crossing, first, layer_gain, route_column, weight_column):
    tp_size = lax.axis_size("tp")
    row_tokens = held.shape[1]
    model_width = held.shape[2]
    received = held.reshape(-1, model_width)
    token_count = received.shape[0]
    present = (jnp.arange(row_tokens)[None, :] < slot_lengths[:, None]).reshape(-1)
    widened = received.astype(jnp.float32)
    normed = (
        widened
        * lax.rsqrt(jnp.mean(widened * widened, axis=1, keepdims=True) + epsilon)
        * layer_gain[None, :]
    ).astype(jnp.bfloat16)
    expert_slots = 5 * token_count // (4 * tp_size)
    taken = slot_plan(route_column, tp_size, expert_slots)
    send_tokens = into_slots(taken, normed).reshape(tp_size, expert_slots, model_width)
    arrived = lax.all_to_all(send_tokens, "tp", split_axis=0, concat_axis=0, tiled=True)
    halves, others = crossing
    if first:
        others, arrived = lax.optimization_barrier((others, arrived))
    gate_up_w, down_w = complete(halves, others)
    hidden_width = down_w.shape[0]
    flattened = arrived.reshape(-1, model_width)
    projected = jnp.dot(flattened, gate_up_w, preferred_element_type=jnp.float32)
    hidden = (jax.nn.silu(projected[:, :hidden_width]) * projected[:, hidden_width:]).astype(
        jnp.bfloat16
    )
    produced = jnp.dot(hidden, down_w, preferred_element_type=jnp.float32).astype(jnp.bfloat16)
    returned = lax.all_to_all(
        produced.reshape(arrived.shape), "tp", split_axis=0, concat_axis=0, tiled=True
    )
    answer = from_slots(taken, returned.reshape(-1, model_width))
    combined = (
        widened
        + (present.astype(jnp.float32) * weight_column)[:, None] * answer.astype(jnp.float32)
    ).astype(jnp.bfloat16)
    return combined.reshape(held.shape)


def per_device(tokens, lengths, plan, owners, gate_up, down, norm_gain, routing, route_weight):
    layer_count = plan.shape[0]
    roll_size = lax.axis_size("roll")
    kept, got = share_halves(gate_up, down)
    home = slot_plan(plan[layer_count - 1, :, 0], roll_size, CAP)
    owner, row_lengths = share_plan(plan, lengths, roll_size)
    first_rows = into_slots(slot_plan(plan[0, :, 0], roll_size, CAP), tokens)
    held = lax.all_to_all(first_rows, "roll", split_axis=0, concat_axis=0, tiled=True)
    crossings, before = [], None
    for layer_index in range(layer_count):
        crossings.append(cross(kept, got, owners[layer_index], before))
        before = crossings[-1][1]
    for layer_index in range(layer_count):
        if layer_index > 0:
            moves = forward_plan(owner[:, layer_index - 1], owner[:, layer_index], roll_size)
            held = forward_rows(held, moves, roll_size)
        held = process_rows(
            held,
            held_lengths(owner[:, layer_index], row_lengths),
            crossings[layer_index],
            layer_index == 0,
            norm_gain[layer_index],
            routing[layer_index, :, 0],
            route_weight[layer_index],
        )
    current = send_home(held, home)
    return current


def solution(mesh):
    in_specs = (
        P(("roll", "tp"), None, None),
        P(("roll", "tp")),
        P(None, ("roll", "tp"), None),
        P(),
        P("roll", "tp", None, None),
        P("roll", "tp", None, None),
        P(),
        P(None, ("roll", "tp"), None),
        P(None, ("roll", "tp")),
    )
    out_specs = P(("roll", "tp"), None, None)
    return jax.shard_map(
        per_device, mesh=mesh, in_specs=in_specs, out_specs=out_specs, check_vma=False
    )
```

time: 224 us -> 204 us (0.911)
  waiting for transfers between devices: 112 us -> 83.8 us
  local copies, waits for them, and re-layouts: 13 us -> 19.1 us
  starting transfers between devices: 36.3 us -> 32.8 us
  other arithmetic: 27.5 us -> 30.3 us
    ppermute x10, waiting for transfers between devices: 51.9 us -> 30.7 us  [swap(): lax.ppermute(value, 'roll', [(place, place ^ distance) for place in range...]
    all_to_all x1, waiting for transfers between devices: 13.5 us -> 0.01 us  [process_rows(): lax.all_to_all(produced.reshape(arrived.shape), 'tp', split_axis=0, conca...]
    all_to_all x5 -> x3, starting transfers between devices: 17.2 us -> 10.5 us  [the longest x1 3.87 us: per_device(): lax.all_to_all(first_rows, 'roll', split_axis=0, concat_axis=0, tiled=True)]
    all_to_all x5 -> x3, waiting for transfers between devices: 21.1 us -> 25.9 us  [the longest x1 25.5 us: share_plan(): got = lax.all_to_all(sent, 'roll', split_axis=0, concat_axis=0, tiled=True)]
    unnamed x34 -> x42, local copies, waits for them, and re-layouts: 4.1 us -> 6.32 us
  transfers between devices with their start and end apart: 18 -> 16, of which waited for: 8 -> 6; matrix products, arithmetic and copies ran while one was open for 15% -> 20% of each run, Pallas kernels for 0% -> 0%
where the time goes in v3:
time: 204 us; the launch traced here: 203 us
  waiting for transfers between devices  83.8 us (41%)
  starting transfers between devices  32.8 us (16%)
  other arithmetic  30.3 us (15%)
  blocking collectives  27.3 us (13%)
  local copies, waits for them, and re-layouts  19.1 us (9%)
  matrix products  5.93 us (3%)
  between operations  3.77 us (2%)
    ppermute x10, waiting for transfers between devices, swap(): lax.ppermute(value, 'roll', [(place, place ^ distance) for place in range...  30.7 us
    all_to_all x2, waiting for transfers between devices, process_rows(): lax.all_to_all(send_tokens, 'tp', split_axis=0, concat_axis=0, tiled=True)  27.2 us
    all_to_all x1, waiting for transfers between devices, share_plan(): got = lax.all_to_all(sent, 'roll', split_axis=0, concat_axis=0, tiled=True)  25.5 us
    all_to_all x1, blocking collectives, process_rows(): lax.all_to_all(produced.reshape(arrived.shape), 'tp', split_axis=0, conca...  18.1 us
    all_to_all x2, starting transfers between devices, process_rows(): lax.all_to_all(send_tokens, 'tp', split_axis=0, concat_axis=0, tiled=True)  10.5 us
    all_to_all x1, blocking collectives, send_home(): lax.all_to_all(combined, 'roll', split_axis=0, concat_axis=0, tiled=True)  9.2 us
    add x4, other arithmetic, complete(): half = half + other  8.17 us
    ppermute x10, starting transfers between devices, swap(): lax.ppermute(value, 'roll', [(place, place ^ distance) for place in range...  7.63 us
  transfers between devices with their start and end apart: 16, of which 6 were waited for; matrix products, arithmetic and copies ran while one was open for 20% of the time, Pallas kernels for 0%

profile of v3, /device:TPU:0, one launch (start us, length us, event | category | flops | bytes accessed | tf_op | source)
XLA Modules:
  0.0 202.9 jit_solution(16858022002478861767)
XLA Ops:
  0.0 3.1 %convert.10 = bf16[1,1,2048,768]{3,2,1,0:T(8,128)(2,1)S(1)} convert(f32[1,1,2048,768]{3,2,1,0:T(8,128)} %param.13) | non-fusion elementwise | flops 1572864 | bytes 9437184 | tf_op jit(solution)/shard_map/convert.5
  9.9 3.9 %all-to-all-start.1 = ((bf16[8,8,2048]{2,1,0:T(8,128)(2,1)}), bf16[8,8,2048]{2,1,0:T(8,128)(2,1)S(1)}, u32[]{:S(2)}, u32[]{:S(2)}) async-start(bf16[8,8,2048]{2,1,0:T(8,128)(2,1)} %copy.15), calls=%async_computation.1 | async-start | bytes 524288 | tf_op jit(solution)/shard_map/all_to_all | solution.py:170
  18.6 3.3 %bitcast_select_fusion = (bf16[1024,768]{1,0:T(8,128)(2,1)}, bf16[1024,768]{1,0:T(8,128)(2,1)}) fusion(bf16[1024,768]{1,0:T(8,128)(2,1)} %collective-permute-done, pred[]{:T(512)S(6)} %eq.277, pred[]{:T(512)S(6)} %eq.276, bf16[1,1,2048,768]{3,2,1,0:T(8,128)(2,1)S(1)} %convert.10, pred[]{:T(512)S(6)} %eq.261, pred[]{:T(512)S(6)} %eq.262, pred[]{:T(512)S(6)} %eq.260), kind=kLoop, calls=%fused_computation.34 | loop fusion | flops 3932160 | bytes 7864325 | tf_op jit(solution)/shard_map/jit(_where)/select_n | solution.py:55
  21.9 2.0 collective-permute-start.1
  24.6 3.2 %all-to-all-start = ((s32[4,1,12]{2,1,0:T(1,128)}), s32[4,1,12]{2,1,0:T(1,128)S(1)}, u32[]{:S(2)}, u32[]{:S(2)}) async-start(s32[4,1,12]{2,1,0:T(1,128)} %broadcast_in_dim.29), calls=%async_computation | async-start | bytes 4096 | tf_op jit(solution)/shard_map/all_to_all | solution.py:85
  28.2 2.7 %bitcast_select_fusion.2 = (bf16[192,2048]{1,0:T(8,128)(2,1)}, bf16[192,2048]{1,0:T(8,128)(2,1)S(1)}) fusion(bf16[192,2048]{1,0:T(8,128)(2,1)} %collective-permute-done.2, pred[]{:T(512)S(6)} %eq.277, pred[]{:T(512)S(6)} %eq.276, bf16[1,1,384,2048]{3,2,1,0:T(8,128)(2,1)} %copy-done, pred[]{:T(512)S(6)} %eq.261, pred[]{:T(512)S(6)} %eq.262, pred[]{:T(512)S(6)} %eq.260), kind=kLoop, calls=%fused_computation.42 | loop fusion | flops 1966080 | bytes 3932165 | tf_op jit(solution)/shard_map/jit(_where)/select_n | solution.py:55
  30.8 2.0 collective-permute-start.3
  34.1 25.5 %all-to-all-done = s32[4,1,12]{2,1,0:T(1,128)S(1)} async-done(((s32[4,1,12]{2,1,0:T(1,128)}), s32[4,1,12]{2,1,0:T(1,128)S(1)}, u32[]{:S(2)}, u32[]{:S(2)}) %all-to-all-start) | async-done | bytes 224 | tf_op jit(solution)/shard_map/all_to_all | solution.py:85
  59.5 6.3 %all-to-all-start.2 = ((bf16[8,10,2048]{2,1,0:T(8,128)(2,1)}), bf16[8,10,2048]{2,1,0:T(8,128)(2,1)S(1)}, u32[]{:S(2)}, u32[]{:S(2)}) async-start(bf16[8,10,2048]{2,1,0:T(8,128)(2,1)} %reshape.238), calls=%async_computation.2 | async-start | bytes 1048576 | tf_op jit(solution)/shard_map/all_to_all | solution.py:140
  65.9 14.7 %all-to-all-done.2 = bf16[8,10,2048]{2,1,0:T(8,128)(2,1)S(1)} async-done(((bf16[8,10,2048]{2,1,0:T(8,128)(2,1)}), bf16[8,10,2048]{2,1,0:T(8,128)(2,1)S(1)}, u32[]{:S(2)}, u32[]{:S(2)}) %all-to-all-start.2) | async-done | bytes 327712 | tf_op jit(solution)/shard_map/all_to_all | solution.py:140
  81.7 2.3 %add.108 = bf16[1024,768]{1,0:T(8,128)(2,1)S(1)} add(bf16[1024,768]{1,0:T(8,128)(2,1)} %get-tuple-element.21, bf16[1024,768]{1,0:T(8,128)(2,1)} %collective-permute-done.1) | non-fusion elementwise | flops 786432 | bytes 4718592 | tf_op jit(solution)/shard_map/add | solution.py:73
  84.2 2.4 %add.110 = bf16[192,2048]{1,0:T(8,128)(2,1)} add(bf16[192,2048]{1,0:T(8,128)(2,1)} %copy-done.3, bf16[192,2048]{1,0:T(8,128)(2,1)S(1)} %copy-done.6) | non-fusion elementwise | flops 393216 | bytes 2359296 | tf_op jit(solution)/shard_map/add | solution.py:73
  88.1 2.0 %collective-permute-start.6 = (bf16[1024,768]{1,0:T(8,128)(2,1)S(1)}, bf16[1024,768]{1,0:T(8,128)(2,1)}, u32[]{:S(2)}, u32[]{:S(2)}) collective-permute-start(bf16[1024,768]{1,0:T(8,128)(2,1)S(1)} %copy-done.1), channel_id=1, source_target_pairs={{0,16},{8,24},{16,0},{24,8},{1,17},{9,25},{17,1},{25,9},{2,18},{10... | collective-permute-start | bytes 4718600 | tf_op jit(solution)/shard_map/ppermute | solution.py:38
  90.1 1.9 reshape.239
  97.1 4.1 %all-to-all-start.3 = ((bf16[8,10,2048]{2,1,0:T(8,128)(2,1)}), bf16[8,10,2048]{2,1,0:T(8,128)(2,1)}, u32[]{:S(2)}, u32[]{:S(2)}) async-start(bf16[8,10,2048]{2,1,0:T(8,128)(2,1)} %reshape.240), calls=%async_computation.3 | async-start | bytes 1048576 | tf_op jit(solution)/shard_map/all_to_all | solution.py:152
  103.5 21.9 %collective-permute-done.6 = bf16[1024,768]{1,0:T(8,128)(2,1)} collective-permute-done((bf16[1024,768]{1,0:T(8,128)(2,1)S(1)}, bf16[1024,768]{1,0:T(8,128)(2,1)}, u32[]{:S(2)}, u32[]{:S(2)}) %collective-permute-start.6) | collective-permute-done | bytes 1572896 | tf_op jit(solution)/shard_map/ppermute | solution.py:38
  130.0 3.4 %all-to-all-start.4 = ((bf16[4,2,8,2048]{3,2,1,0:T(8,128)(2,1)}), bf16[4,2,8,2048]{3,2,1,0:T(8,128)(2,1)S(1)}, u32[]{:S(2)}, u32[]{:S(2)}) async-start(bf16[4,2,8,2048]{3,2,1,0:T(8,128)(2,1)} %bitcast.78), calls=%async_computation.4 | async-start | bytes 524288 | tf_op jit(solution)/shard_map/all_to_all | solution.py:115
  133.5 8.8 %collective-permute-done.8 = bf16[192,2048]{1,0:T(8,128)(2,1)} collective-permute-done((bf16[192,2048]{1,0:T(8,128)(2,1)}, bf16[192,2048]{1,0:T(8,128)(2,1)}, u32[]{:S(2)}, u32[]{:S(2)}) %collective-permute-start.8) | collective-permute-done | bytes 786464 | tf_op jit(solution)/shard_map/ppermute | solution.py:38
  148.3 1.9 reshape.244
  150.2 4.2 %all-to-all-start.5 = ((bf16[8,10,2048]{2,1,0:T(8,128)(2,1)}), bf16[8,10,2048]{2,1,0:T(8,128)(2,1)}, u32[]{:S(2)}, u32[]{:S(2)}) async-start(bf16[8,10,2048]{2,1,0:T(8,128)(2,1)} %reshape.244), calls=%async_computation.5 | async-start | bytes 1048576 | tf_op jit(solution)/shard_map/all_to_all | solution.py:140
  154.4 2.4 %broadcast_select_fusion.6 = (bf16[192,2048]{1,0:T(8,128)(2,1)}, bf16[192,2048]{1,0:T(8,128)(2,1)}) fusion(bf16[192,2048]{1,0:T(8,128)(2,1)} %collective-permute-done.9, bf16[192,2048]{1,0:T(8,128)(2,1)S(1)} %add.116, pred[]{:T(512)S(6)} %eq.261), kind=kLoop, calls=%fused_computation.46 | loop fusion | flops 786432 | bytes 3145729 | tf_op jit(solution)/shard_map/jit(_where)/select_n | solution.py:76
  156.8 12.6 %all-to-all-done.5 = bf16[8,10,2048]{2,1,0:T(8,128)(2,1)} async-done(((bf16[8,10,2048]{2,1,0:T(8,128)(2,1)}), bf16[8,10,2048]{2,1,0:T(8,128)(2,1)}, u32[]{:S(2)}, u32[]{:S(2)}) %all-to-all-start.5) | async-done | bytes 327712 | tf_op jit(solution)/shard_map/all_to_all | solution.py:140
  174.1 18.1 %all_to_all.44 = bf16[8,10,2048]{2,1,0:T(8,128)(2,1)S(1)} all-to-all(bf16[8,10,2048]{2,1,0:T(8,128)(2,1)S(1)} %reshape.246), channel_id=1, replica_groups=mesh['roll'=4,'tp'=8] {'tp'}, dimensions={0} | all-to-all | bytes 655360 | tf_op jit(solution)/shard_map/all_to_all | solution.py:152
  192.6 9.2 %all_to_all.45 = bf16[8,8,2048]{2,1,0:T(8,128)(2,1)S(1)} all-to-all(bf16[8,8,2048]{2,1,0:T(8,128)(2,1)S(1)} %fusion.17), channel_id=1, replica_groups=mesh['roll'=4,'tp'=8] {'roll'}, dimensions={0} | all-to-all | bytes 524288 | tf_op jit(solution)/shard_map/all_to_all | solution.py:120
  (127 shorter events, 37.4 us)
Async XLA Ops:
  3.1 2.5 %copy-start.2 = (f32[1,1,384,2048]{3,2,1,0:T(8,128)S(1)}, f32[1,1,384,2048]{3,2,1,0:T(8,128)}, u32[]{:S(2)}) copy-start(f32[1,1,384,2048]{3,2,1,0:T(8,128)} %param.14) | copy-start | bytes 9437188
  4.4 14.2 %collective-permute-start = (bf16[1024,768]{1,0:T(8,128)(2,1)}, bf16[1024,768]{1,0:T(8,128)(2,1)}, u32[]{:S(2)}, u32[]{:S(2)}) collective-permute-start(bf16[1024,768]{1,0:T(8,128)(2,1)} %select_bitcast_fusion), channel_id=1, source_target_pairs={{0,8},{8,0},{16,24},{24,16},{1,9},{9,1},{17,25},{25,17},{2,10},{10... | collective-permute-start | bytes 4718600 | tf_op jit(solution)/shard_map/ppermute | solution.py:38
  6.9 6.8 %copy-start.14 = (s32[4]{0:T(128)S(1)}, s32[4]{0:T(128)}, u32[]{:S(2)}) copy-start(s32[4]{0:T(128)} %param.12) | copy-start | bytes 52
  6.9 11.4 %copy-start.16 = (s32[4]{0:T(128)S(1)}, s32[4]{0:T(128)}, u32[]{:S(2)}) copy-start(s32[4]{0:T(128)} %param.10) | copy-start | bytes 52
  6.9 11.4 %copy-start.13 = (s32[2,64,1]{1,2,0:T(1,128)S(1)}, s32[2,64,1]{1,2,0:T(1,128)}, u32[]{:S(2)}) copy-start(s32[2,64,1]{1,2,0:T(1,128)} %param.16) | copy-start | bytes 1540
  7.0 11.6 %copy-start.11 = (f32[2,2048]{1,0:T(2,128)S(1)}, f32[2,2048]{1,0:T(2,128)}, u32[]{:S(2)}) copy-start(f32[2,2048]{1,0:T(2,128)} %param.15) | copy-start | bytes 49156
  8.0 20.2 %collective-permute-start.2 = (bf16[192,2048]{1,0:T(8,128)(2,1)}, bf16[192,2048]{1,0:T(8,128)(2,1)}, u32[]{:S(2)}, u32[]{:S(2)}) collective-permute-start(bf16[192,2048]{1,0:T(8,128)(2,1)} %select_bitcast_fusion.1), channel_id=1, source_target_pairs={{0,8},{8,0},{16,24},{24,16},{1,9},{9,1},{17,25},{25,17},{2,10},{10... | collective-permute-start | bytes 2359304 | tf_op jit(solution)/shard_map/ppermute | solution.py:38
  9.9 14.1 %all-to-all-start.1 = ((bf16[8,8,2048]{2,1,0:T(8,128)(2,1)}), bf16[8,8,2048]{2,1,0:T(8,128)(2,1)S(1)}, u32[]{:S(2)}, u32[]{:S(2)}) async-start(bf16[8,8,2048]{2,1,0:T(8,128)(2,1)} %copy.15), calls=%async_computation.1 | async-start | bytes 524288 | tf_op jit(solution)/shard_map/all_to_all | solution.py:170
  21.9 59.6 %collective-permute-start.1 = (bf16[1024,768]{1,0:T(8,128)(2,1)}, bf16[1024,768]{1,0:T(8,128)(2,1)}, u32[]{:S(2)}, u32[]{:S(2)}) collective-permute-start(bf16[1024,768]{1,0:T(8,128)(2,1)} %get-tuple-element.21), channel_id=1, source_target_pairs={{0,16},{8,24},{16,0},{24,8},{1,17},{9,25},{17,1},{25,9},{2,18},{10... | collective-permute-start | bytes 4718600 | tf_op jit(solution)/shard_map/ppermute | solution.py:38
  24.6 35.0 %all-to-all-start = ((s32[4,1,12]{2,1,0:T(1,128)}), s32[4,1,12]{2,1,0:T(1,128)S(1)}, u32[]{:S(2)}, u32[]{:S(2)}) async-start(s32[4,1,12]{2,1,0:T(1,128)} %broadcast_in_dim.29), calls=%async_computation | async-start | bytes 4096 | tf_op jit(solution)/shard_map/all_to_all | solution.py:85
  30.8 50.8 %copy-start.3 = (bf16[192,2048]{1,0:T(8,128)(2,1)}, bf16[192,2048]{1,0:T(8,128)(2,1)S(1)}, u32[]{:S(2)}) copy-start(bf16[192,2048]{1,0:T(8,128)(2,1)S(1)} %get-tuple-element.27) | copy-start | bytes 2359300
  30.8 49.8 %collective-permute-start.3 = (bf16[192,2048]{1,0:T(8,128)(2,1)S(1)}, bf16[192,2048]{1,0:T(8,128)(2,1)S(1)}, u32[]{:S(2)}, u32[]{:S(2)}) collective-permute-start(bf16[192,2048]{1,0:T(8,128)(2,1)S(1)} %get-tuple-element.27), channel_id=1, source_target_pairs={{0,16},{8,24},{16,0},{24,8},{1,17},{9,25},{17,1},{25,9},{2,18},{10... | collective-permute-start | bytes 2359304 | tf_op jit(solution)/shard_map/ppermute | solution.py:38
  59.5 21.0 %all-to-all-start.2 = ((bf16[8,10,2048]{2,1,0:T(8,128)(2,1)}), bf16[8,10,2048]{2,1,0:T(8,128)(2,1)S(1)}, u32[]{:S(2)}, u32[]{:S(2)}) async-start(bf16[8,10,2048]{2,1,0:T(8,128)(2,1)} %reshape.238), calls=%async_computation.2 | async-start | bytes 1048576 | tf_op jit(solution)/shard_map/all_to_all | solution.py:140
  84.1 4.0 %copy-start.1 = (bf16[1024,768]{1,0:T(8,128)(2,1)S(1)}, bf16[1024,768]{1,0:T(8,128)(2,1)}, u32[]{:S(2)}) copy-start(bf16[1024,768]{1,0:T(8,128)(2,1)} %get-tuple-element.13) | copy-start | bytes 4718596
  84.1 9.4 %collective-permute-start.4 = (bf16[1024,768]{1,0:T(8,128)(2,1)S(1)}, bf16[1024,768]{1,0:T(8,128)(2,1)}, u32[]{:S(2)}, u32[]{:S(2)}) collective-permute-start(bf16[1024,768]{1,0:T(8,128)(2,1)S(1)} %add.108), channel_id=1, source_target_pairs={{0,8},{8,0},{16,24},{24,16},{1,9},{9,1},{17,25},{25,17},{2,10},{10... | collective-permute-start | bytes 4718600 | tf_op jit(solution)/shard_map/ppermute | solution.py:38
  86.6 5.4 %collective-permute-start.5 = (bf16[192,2048]{1,0:T(8,128)(2,1)}, bf16[192,2048]{1,0:T(8,128)(2,1)}, u32[]{:S(2)}, u32[]{:S(2)}) collective-permute-start(bf16[192,2048]{1,0:T(8,128)(2,1)} %add.110), channel_id=1, source_target_pairs={{0,8},{8,0},{16,24},{24,16},{1,9},{9,1},{17,25},{25,17},{2,10},{10... | collective-permute-start | bytes 2359304 | tf_op jit(solution)/shard_map/ppermute | solution.py:38
  88.1 37.3 %collective-permute-start.6 = (bf16[1024,768]{1,0:T(8,128)(2,1)S(1)}, bf16[1024,768]{1,0:T(8,128)(2,1)}, u32[]{:S(2)}, u32[]{:S(2)}) collective-permute-start(bf16[1024,768]{1,0:T(8,128)(2,1)S(1)} %copy-done.1), channel_id=1, source_target_pairs={{0,16},{8,24},{16,0},{24,8},{1,17},{9,25},{17,1},{25,9},{2,18},{10... | collective-permute-start | bytes 4718600 | tf_op jit(solution)/shard_map/ppermute | solution.py:38
  96.2 6.5 %copy-start.15 = (f32[2,64]{1,0:T(2,128)S(1)}, f32[2,64]{1,0:T(2,128)}, u32[]{:S(2)}) copy-start(f32[2,64]{1,0:T(2,128)} %param.17) | copy-start | bytes 1540
  97.1 30.1 %all-to-all-start.3 = ((bf16[8,10,2048]{2,1,0:T(8,128)(2,1)}), bf16[8,10,2048]{2,1,0:T(8,128)(2,1)}, u32[]{:S(2)}, u32[]{:S(2)}) async-start(bf16[8,10,2048]{2,1,0:T(8,128)(2,1)} %reshape.240), calls=%async_computation.3 | async-start | bytes 1048576 | tf_op jit(solution)/shard_map/all_to_all | solution.py:152
  102.8 39.5 %collective-permute-start.8 = (bf16[192,2048]{1,0:T(8,128)(2,1)}, bf16[192,2048]{1,0:T(8,128)(2,1)}, u32[]{:S(2)}, u32[]{:S(2)}) collective-permute-start(bf16[192,2048]{1,0:T(8,128)(2,1)} %get-tuple-element.14), channel_id=1, source_target_pairs={{0,16},{8,24},{16,0},{24,8},{1,17},{9,25},{17,1},{25,9},{2,18},{10... | collective-permute-start | bytes 2359304 | tf_op jit(solution)/shard_map/ppermute | solution.py:38
  127.2 43.3 %collective-permute-start.7 = (bf16[1024,768]{1,0:T(8,128)(2,1)S(1)}, bf16[1024,768]{1,0:T(8,128)(2,1)}, u32[]{:S(2)}, u32[]{:S(2)}) collective-permute-start(bf16[1024,768]{1,0:T(8,128)(2,1)S(1)} %add.114), channel_id=1, source_target_pairs={{0,8},{8,0},{16,24},{24,16},{1,9},{9,1},{17,25},{25,17},{2,10},{10... | collective-permute-start | bytes 4718600 | tf_op jit(solution)/shard_map/ppermute | solution.py:38
  130.0 14.4 %all-to-all-start.4 = ((bf16[4,2,8,2048]{3,2,1,0:T(8,128)(2,1)}), bf16[4,2,8,2048]{3,2,1,0:T(8,128)(2,1)S(1)}, u32[]{:S(2)}, u32[]{:S(2)}) async-start(bf16[4,2,8,2048]{3,2,1,0:T(8,128)(2,1)} %bitcast.78), calls=%async_computation.4 | async-start | bytes 524288 | tf_op jit(solution)/shard_map/all_to_all | solution.py:115
  143.9 10.5 %collective-permute-start.9 = (bf16[192,2048]{1,0:T(8,128)(2,1)S(1)}, bf16[192,2048]{1,0:T(8,128)(2,1)}, u32[]{:S(2)}, u32[]{:S(2)}) collective-permute-start(bf16[192,2048]{1,0:T(8,128)(2,1)S(1)} %add.116), channel_id=1, source_target_pairs={{0,8},{8,0},{16,24},{24,16},{1,9},{9,1},{17,25},{25,17},{2,10},{10... | collective-permute-start | bytes 2359304 | tf_op jit(solution)/shard_map/ppermute | solution.py:38
  150.2 19.1 %all-to-all-start.5 = ((bf16[8,10,2048]{2,1,0:T(8,128)(2,1)}), bf16[8,10,2048]{2,1,0:T(8,128)(2,1)}, u32[]{:S(2)}, u32[]{:S(2)}) async-start(bf16[8,10,2048]{2,1,0:T(8,128)(2,1)} %reshape.244), calls=%async_computation.5 | async-start | bytes 1048576 | tf_op jit(solution)/shard_map/all_to_all | solution.py:140
  (9 other events, 13.1 us)

commit v4 on v3

--- a/solution.py
+++ b/solution.py
@@ -55,8 +55,7 @@
         jnp.where(owner == me, mine, jnp.where(owner == me ^ 1, theirs, jnp.zeros_like(mine)))
         for mine, theirs in zip(kept, got)
     ]
-    if before is not None:
-        halves, _ = lax.optimization_barrier((halves, before))
+    halves, _ = lax.optimization_barrier((halves, before))
     others = [jnp.zeros_like(half) for half in halves]
     distance = 2
     while distance < lax.axis_size("roll"):
@@ -168,7 +167,7 @@
     owner, row_lengths = share_plan(plan, lengths, roll_size)
     first_rows = into_slots(slot_plan(plan[0, :, 0], roll_size, CAP), tokens)
     held = lax.all_to_all(first_rows, "roll", split_axis=0, concat_axis=0, tiled=True)
-    crossings, before = [], None
+    crossings, before = [], (owner, row_lengths, held)
     for layer_index in range(layer_count):
         crossings.append(cross(kept, got, owners[layer_index], before))
         before = crossings[-1][1]

time: 204 us -> 203 us (level)
  local copies, waits for them, and re-layouts: 19.1 us -> 14.8 us
  starting transfers between devices: 32.8 us -> 35.8 us
  waiting for transfers between devices: 83.8 us -> 86.7 us
    ppermute x10, waiting for transfers between devices: 30.7 us -> 59.4 us  [swap(): lax.ppermute(value, 'roll', [(place, place ^ distance) for place in range...]
    all_to_all x1, waiting for transfers between devices: 25.5 us -> 0.01 us  [share_plan(): got = lax.all_to_all(sent, 'roll', split_axis=0, concat_axis=0, tiled=True)]
    all_to_all x1, starting transfers between devices: 4.15 us -> 6.27 us  [process_rows(): lax.all_to_all(produced.reshape(arrived.shape), 'tp', split_axis=0, conca...]
    all_to_all x2, starting transfers between devices: 10.5 us -> 12.5 us  [process_rows(): lax.all_to_all(send_tokens, 'tp', split_axis=0, concat_axis=0, tiled=True)]
  transfers between devices with their start and end apart: 16 -> 16, of which waited for: 6 -> 6; matrix products, arithmetic and copies ran while one was open for 20% -> 18% of each run, Pallas kernels for 0% -> 0%
where the time goes in v4:
time: 203 us; the launch traced here: 202 us
  waiting for transfers between devices  86.7 us (43%)
  starting transfers between devices  35.8 us (18%)
  other arithmetic  29.4 us (14%)
  blocking collectives  26.9 us (13%)
  local copies, waits for them, and re-layouts  14.8 us (7%)
  matrix products  4.39 us (2%)
  between operations  3.76 us (2%)
    ppermute x10, waiting for transfers between devices, swap(): lax.ppermute(value, 'roll', [(place, place ^ distance) for place in range...  59.4 us
    all_to_all x2, waiting for transfers between devices, process_rows(): lax.all_to_all(send_tokens, 'tp', split_axis=0, concat_axis=0, tiled=True)  27.2 us
    all_to_all x1, blocking collectives, process_rows(): lax.all_to_all(produced.reshape(arrived.shape), 'tp', split_axis=0, conca...  18.1 us
    all_to_all x2, starting transfers between devices, process_rows(): lax.all_to_all(send_tokens, 'tp', split_axis=0, concat_axis=0, tiled=True)  12.5 us
    all_to_all x1, blocking collectives, send_home(): lax.all_to_all(combined, 'roll', split_axis=0, concat_axis=0, tiled=True)  8.77 us
    select_n x4, other arithmetic, complete(): jnp.where(upper, other, half)  7.14 us
    add x4, other arithmetic, complete(): half = half + other  6.47 us
    select_n x2, other arithmetic, cross(): jnp.where(owner == me, mine, jnp.where(owner == me ^ 1, theirs, jnp.zeros...  6.27 us
  transfers between devices with their start and end apart: 16, of which 6 were waited for; matrix products, arithmetic and copies ran while one was open for 18% of the time, Pallas kernels for 0%

profile of v4, /device:TPU:0, one launch (start us, length us, event | category | flops | bytes accessed | tf_op | source)
XLA Modules:
  0.0 201.8 jit_solution(14525525016751189502)
XLA Ops:
  3.2 4.2 %all-to-all-start = ((s32[4,1,12]{2,1,0:T(1,128)}), s32[4,1,12]{2,1,0:T(1,128)S(1)}, u32[]{:S(2)}, u32[]{:S(2)}) async-start(s32[4,1,12]{2,1,0:T(1,128)} %broadcast_in_dim.29), calls=%async_computation | async-start | bytes 4096 | tf_op jit(solution)/shard_map/all_to_all | solution.py:84
  7.5 2.3 %convert.11 = bf16[1,1,384,2048]{3,2,1,0:T(8,128)(2,1)S(1)} convert(f32[1,1,384,2048]{3,2,1,0:T(8,128)} %param.14) | non-fusion elementwise | flops 786432 | bytes 4718592 | tf_op jit(solution)/shard_map/convert.3
  19.2 3.4 %all-to-all-start.1 = ((bf16[8,8,2048]{2,1,0:T(8,128)(2,1)}), bf16[8,8,2048]{2,1,0:T(8,128)(2,1)S(1)}, u32[]{:S(2)}, u32[]{:S(2)}) async-start(bf16[8,8,2048]{2,1,0:T(8,128)(2,1)} %copy.15), calls=%async_computation.1 | async-start | bytes 524288 | tf_op jit(solution)/shard_map/all_to_all | solution.py:169
  22.7 2.9 %bitcast_select_fusion.2 = (bf16[192,2048]{1,0:T(8,128)(2,1)}, bf16[192,2048]{1,0:T(8,128)(2,1)}) fusion(bf16[192,2048]{1,0:T(8,128)(2,1)} %collective-permute-done.1, pred[]{:T(512)S(6)} %eq.277, pred[]{:T(512)S(6)} %eq.276, bf16[1,1,384,2048]{3,2,1,0:T(8,128)(2,1)} %copy-done, pred[]{:T(512)S(6)} %eq.261, pred[]{:T(512)S(6)} %eq.262, pred[]{:T(512)S(6)} %eq.260), kind=kLoop, calls=%fused_computation.42 | loop fusion | flops 1966080 | bytes 3932165 | tf_op jit(solution)/shard_map/jit(_where)/select_n | solution.py:55
  25.7 3.3 %bitcast_select_fusion = (bf16[1024,768]{1,0:T(8,128)(2,1)}, bf16[1024,768]{1,0:T(8,128)(2,1)}) fusion(bf16[1024,768]{1,0:T(8,128)(2,1)} %collective-permute-done, pred[]{:T(512)S(6)} %eq.277, pred[]{:T(512)S(6)} %eq.276, bf16[1,1,2048,768]{3,2,1,0:T(8,128)(2,1)S(1)} %convert.10, pred[]{:T(512)S(6)} %eq.261, pred[]{:T(512)S(6)} %eq.262, pred[]{:T(512)S(6)} %eq.260), kind=kLoop, calls=%fused_computation.34 | loop fusion | flops 3932160 | bytes 7864325 | tf_op jit(solution)/shard_map/jit(_where)/select_n | solution.py:55
  29.0 2.0 collective-permute-start.2
  32.7 6.3 %all-to-all-start.2 = ((bf16[8,10,2048]{2,1,0:T(8,128)(2,1)}), bf16[8,10,2048]{2,1,0:T(8,128)(2,1)S(1)}, u32[]{:S(2)}, u32[]{:S(2)}) async-start(bf16[8,10,2048]{2,1,0:T(8,128)(2,1)} %reshape.238), calls=%async_computation.2 | async-start | bytes 1048576 | tf_op jit(solution)/shard_map/all_to_all | solution.py:139
  38.9 14.5 %all-to-all-done.2 = bf16[8,10,2048]{2,1,0:T(8,128)(2,1)S(1)} async-done(((bf16[8,10,2048]{2,1,0:T(8,128)(2,1)}), bf16[8,10,2048]{2,1,0:T(8,128)(2,1)S(1)}, u32[]{:S(2)}, u32[]{:S(2)}) %all-to-all-start.2) | async-done | bytes 327712 | tf_op jit(solution)/shard_map/all_to_all | solution.py:139
  53.5 29.4 %collective-permute-done.3 = bf16[192,2048]{1,0:T(8,128)(2,1)S(1)} collective-permute-done((bf16[192,2048]{1,0:T(8,128)(2,1)}, bf16[192,2048]{1,0:T(8,128)(2,1)S(1)}, u32[]{:S(2)}, u32[]{:S(2)}) %collective-permute-start.3) | collective-permute-done | bytes 786464 | tf_op jit(solution)/shard_map/ppermute | solution.py:38
  83.8 1.9 add.108
  88.2 1.9 reshape.239
  90.0 1.7 collective-permute-start.6
  93.2 1.7 broadcast_select_fusion.3
  96.9 6.3 %all-to-all-start.3 = ((bf16[8,10,2048]{2,1,0:T(8,128)(2,1)}), bf16[8,10,2048]{2,1,0:T(8,128)(2,1)}, u32[]{:S(2)}, u32[]{:S(2)}) async-start(bf16[8,10,2048]{2,1,0:T(8,128)(2,1)} %reshape.240), calls=%async_computation.3 | async-start | bytes 1048576 | tf_op jit(solution)/shard_map/all_to_all | solution.py:151
  106.1 21.3 %collective-permute-done.6 = bf16[1024,768]{1,0:T(8,128)(2,1)} collective-permute-done((bf16[1024,768]{1,0:T(8,128)(2,1)S(1)}, bf16[1024,768]{1,0:T(8,128)(2,1)}, u32[]{:S(2)}, u32[]{:S(2)}) %collective-permute-start.6) | collective-permute-done | bytes 1572896 | tf_op jit(solution)/shard_map/ppermute | solution.py:38
  127.4 1.8 add.114
  132.1 3.4 %all-to-all-start.4 = ((bf16[4,2,8,2048]{3,2,1,0:T(8,128)(2,1)}), bf16[4,2,8,2048]{3,2,1,0:T(8,128)(2,1)S(1)}, u32[]{:S(2)}, u32[]{:S(2)}) async-start(bf16[4,2,8,2048]{3,2,1,0:T(8,128)(2,1)} %bitcast.78), calls=%async_computation.4 | async-start | bytes 524288 | tf_op jit(solution)/shard_map/all_to_all | solution.py:114
  135.5 8.8 %collective-permute-done.8 = bf16[192,2048]{1,0:T(8,128)(2,1)} collective-permute-done((bf16[192,2048]{1,0:T(8,128)(2,1)}, bf16[192,2048]{1,0:T(8,128)(2,1)}, u32[]{:S(2)}, u32[]{:S(2)}) %collective-permute-start.8) | collective-permute-done | bytes 786464 | tf_op jit(solution)/shard_map/ppermute | solution.py:38
  144.3 1.6 add.116
  148.3 6.3 %all-to-all-start.5 = ((bf16[8,10,2048]{2,1,0:T(8,128)(2,1)}), bf16[8,10,2048]{2,1,0:T(8,128)(2,1)S(1)}, u32[]{:S(2)}, u32[]{:S(2)}) async-start(bf16[8,10,2048]{2,1,0:T(8,128)(2,1)} %reshape.244), calls=%async_computation.5 | async-start | bytes 1048576 | tf_op jit(solution)/shard_map/all_to_all | solution.py:139
  154.6 2.4 %broadcast_select_fusion.6 = (bf16[192,2048]{1,0:T(8,128)(2,1)}, bf16[192,2048]{1,0:T(8,128)(2,1)}) fusion(bf16[192,2048]{1,0:T(8,128)(2,1)} %collective-permute-done.9, bf16[192,2048]{1,0:T(8,128)(2,1)S(1)} %add.116, pred[]{:T(512)S(6)} %eq.261), kind=kLoop, calls=%fused_computation.46 | loop fusion | flops 786432 | bytes 3145729 | tf_op jit(solution)/shard_map/jit(_where)/select_n | solution.py:75
  157.0 12.7 %all-to-all-done.5 = bf16[8,10,2048]{2,1,0:T(8,128)(2,1)S(1)} async-done(((bf16[8,10,2048]{2,1,0:T(8,128)(2,1)}), bf16[8,10,2048]{2,1,0:T(8,128)(2,1)S(1)}, u32[]{:S(2)}, u32[]{:S(2)}) %all-to-all-start.5) | async-done | bytes 327712 | tf_op jit(solution)/shard_map/all_to_all | solution.py:139
  173.4 18.1 %all_to_all.44 = bf16[8,10,2048]{2,1,0:T(8,128)(2,1)S(1)} all-to-all(bf16[8,10,2048]{2,1,0:T(8,128)(2,1)S(1)} %reshape.246), channel_id=1, replica_groups=mesh['roll'=4,'tp'=8] {'tp'}, dimensions={0} | all-to-all | bytes 655360 | tf_op jit(solution)/shard_map/all_to_all | solution.py:151
  191.9 8.8 %all_to_all.45 = bf16[8,8,2048]{2,1,0:T(8,128)(2,1)S(1)} all-to-all(bf16[8,8,2048]{2,1,0:T(8,128)(2,1)S(1)} %fusion.17), channel_id=1, replica_groups=mesh['roll'=4,'tp'=8] {'roll'}, dimensions={0} | all-to-all | bytes 524288 | tf_op jit(solution)/shard_map/all_to_all | solution.py:119
  (127 shorter events, 31.3 us)
Async XLA Ops:
  3.2 15.9 %all-to-all-start = ((s32[4,1,12]{2,1,0:T(1,128)}), s32[4,1,12]{2,1,0:T(1,128)S(1)}, u32[]{:S(2)}, u32[]{:S(2)}) async-start(s32[4,1,12]{2,1,0:T(1,128)} %broadcast_in_dim.29), calls=%async_computation | async-start | bytes 4096 | tf_op jit(solution)/shard_map/all_to_all | solution.py:84
  7.5 4.6 %copy-start.1 = (f32[1,1,2048,768]{3,2,1,0:T(8,128)S(1)}, f32[1,1,2048,768]{3,2,1,0:T(8,128)}, u32[]{:S(2)}) copy-start(f32[1,1,2048,768]{3,2,1,0:T(8,128)} %param.13) | copy-start | bytes 18874372
  11.2 11.6 %collective-permute-start.1 = (bf16[192,2048]{1,0:T(8,128)(2,1)}, bf16[192,2048]{1,0:T(8,128)(2,1)}, u32[]{:S(2)}, u32[]{:S(2)}) collective-permute-start(bf16[192,2048]{1,0:T(8,128)(2,1)} %select_bitcast_fusion.1), channel_id=1, source_target_pairs={{0,8},{8,0},{16,24},{24,16},{1,9},{9,1},{17,25},{25,17},{2,10},{10... | collective-permute-start | bytes 2359304 | tf_op jit(solution)/shard_map/ppermute | solution.py:38
  12.4 5.3 %copy-start.11 = (bf16[4,8,2048]{2,1,0:T(8,128)(2,1)S(1)}, bf16[4,8,2048]{2,1,0:T(8,128)(2,1)}, u32[]{:S(2)}) copy-start(bf16[4,8,2048]{2,1,0:T(8,128)(2,1)} %param.9) | copy-start | bytes 393220
  12.4 5.4 %copy-start.13 = (s32[2,4,1]{1,2,0:T(1,128)S(1)}, s32[2,4,1]{1,2,0:T(1,128)}, u32[]{:S(2)}) copy-start(s32[2,4,1]{1,2,0:T(1,128)} %param.11) | copy-start | bytes 100
  13.7 11.9 %collective-permute-start = (bf16[1024,768]{1,0:T(8,128)(2,1)}, bf16[1024,768]{1,0:T(8,128)(2,1)}, u32[]{:S(2)}, u32[]{:S(2)}) collective-permute-start(bf16[1024,768]{1,0:T(8,128)(2,1)} %select_bitcast_fusion), channel_id=1, source_target_pairs={{0,8},{8,0},{16,24},{24,16},{1,9},{9,1},{17,25},{25,17},{2,10},{10... | collective-permute-start | bytes 4718600 | tf_op jit(solution)/shard_map/ppermute | solution.py:38
  19.2 9.9 %all-to-all-start.1 = ((bf16[8,8,2048]{2,1,0:T(8,128)(2,1)}), bf16[8,8,2048]{2,1,0:T(8,128)(2,1)S(1)}, u32[]{:S(2)}, u32[]{:S(2)}) async-start(bf16[8,8,2048]{2,1,0:T(8,128)(2,1)} %copy.15), calls=%async_computation.1 | async-start | bytes 524288 | tf_op jit(solution)/shard_map/all_to_all | solution.py:169
  25.7 5.3 %copy-start.12 = (f32[2,2048]{1,0:T(2,128)S(1)}, f32[2,2048]{1,0:T(2,128)}, u32[]{:S(2)}) copy-start(f32[2,2048]{1,0:T(2,128)} %param.15) | copy-start | bytes 49156
  29.0 54.8 %copy-start.3 = (bf16[1024,768]{1,0:T(8,128)(2,1)S(1)}, bf16[1024,768]{1,0:T(8,128)(2,1)}, u32[]{:S(2)}) copy-start(bf16[1024,768]{1,0:T(8,128)(2,1)} %get-tuple-element.12) | copy-start | bytes 4718596
  29.0 54.8 %collective-permute-start.2 = (bf16[1024,768]{1,0:T(8,128)(2,1)}, bf16[1024,768]{1,0:T(8,128)(2,1)}, u32[]{:S(2)}, u32[]{:S(2)}) collective-permute-start(bf16[1024,768]{1,0:T(8,128)(2,1)} %get-tuple-element.12), channel_id=1, source_target_pairs={{0,16},{8,24},{16,0},{24,8},{1,17},{9,25},{17,1},{25,9},{2,18},{10... | collective-permute-start | bytes 4718600 | tf_op jit(solution)/shard_map/ppermute | solution.py:38
  31.4 51.5 %collective-permute-start.3 = (bf16[192,2048]{1,0:T(8,128)(2,1)}, bf16[192,2048]{1,0:T(8,128)(2,1)S(1)}, u32[]{:S(2)}, u32[]{:S(2)}) collective-permute-start(bf16[192,2048]{1,0:T(8,128)(2,1)} %get-tuple-element.13), channel_id=1, source_target_pairs={{0,16},{8,24},{16,0},{24,8},{1,17},{9,25},{17,1},{25,9},{2,18},{10... | collective-permute-start | bytes 2359304 | tf_op jit(solution)/shard_map/ppermute | solution.py:38
  32.7 20.8 %all-to-all-start.2 = ((bf16[8,10,2048]{2,1,0:T(8,128)(2,1)}), bf16[8,10,2048]{2,1,0:T(8,128)(2,1)S(1)}, u32[]{:S(2)}, u32[]{:S(2)}) async-start(bf16[8,10,2048]{2,1,0:T(8,128)(2,1)} %reshape.238), calls=%async_computation.2 | async-start | bytes 1048576 | tf_op jit(solution)/shard_map/all_to_all | solution.py:139
  53.5 29.4 %copy-start.5 = (bf16[8,10,2048]{2,1,0:T(8,128)(2,1)}, bf16[8,10,2048]{2,1,0:T(8,128)(2,1)S(1)}, u32[]{:S(2)}) copy-start(bf16[8,10,2048]{2,1,0:T(8,128)(2,1)S(1)} %all-to-all-done.2) | copy-start | bytes 983044
  53.5 32.2 %copy-start.4 = (bf16[192,2048]{1,0:T(8,128)(2,1)S(1)}, bf16[192,2048]{1,0:T(8,128)(2,1)}, u32[]{:S(2)}) copy-start(bf16[192,2048]{1,0:T(8,128)(2,1)} %get-tuple-element.13) | copy-start | bytes 2359300
  85.6 7.6 %collective-permute-start.4 = (bf16[1024,768]{1,0:T(8,128)(2,1)S(1)}, bf16[1024,768]{1,0:T(8,128)(2,1)}, u32[]{:S(2)}, u32[]{:S(2)}) collective-permute-start(bf16[1024,768]{1,0:T(8,128)(2,1)S(1)} %add.108), channel_id=1, source_target_pairs={{0,8},{8,0},{16,24},{24,16},{1,9},{9,1},{17,25},{25,17},{2,10},{10... | collective-permute-start | bytes 4718600 | tf_op jit(solution)/shard_map/ppermute | solution.py:38
  86.9 4.8 %collective-permute-start.5 = (bf16[192,2048]{1,0:T(8,128)(2,1)}, bf16[192,2048]{1,0:T(8,128)(2,1)}, u32[]{:S(2)}, u32[]{:S(2)}) collective-permute-start(bf16[192,2048]{1,0:T(8,128)(2,1)} %add.110), channel_id=1, source_target_pairs={{0,8},{8,0},{16,24},{24,16},{1,9},{9,1},{17,25},{25,17},{2,10},{10... | collective-permute-start | bytes 2359304 | tf_op jit(solution)/shard_map/ppermute | solution.py:38
  90.0 37.4 %collective-permute-start.6 = (bf16[1024,768]{1,0:T(8,128)(2,1)S(1)}, bf16[1024,768]{1,0:T(8,128)(2,1)}, u32[]{:S(2)}, u32[]{:S(2)}) collective-permute-start(bf16[1024,768]{1,0:T(8,128)(2,1)S(1)} %copy-done.2), channel_id=1, source_target_pairs={{0,16},{8,24},{16,0},{24,8},{1,17},{9,25},{17,1},{25,9},{2,18},{10... | collective-permute-start | bytes 4718600 | tf_op jit(solution)/shard_map/ppermute | solution.py:38
  96.0 8.9 %copy-start.16 = (f32[2,64]{1,0:T(2,128)S(1)}, f32[2,64]{1,0:T(2,128)}, u32[]{:S(2)}) copy-start(f32[2,64]{1,0:T(2,128)} %param.17) | copy-start | bytes 1540
  96.9 32.4 %all-to-all-start.3 = ((bf16[8,10,2048]{2,1,0:T(8,128)(2,1)}), bf16[8,10,2048]{2,1,0:T(8,128)(2,1)}, u32[]{:S(2)}, u32[]{:S(2)}) async-start(bf16[8,10,2048]{2,1,0:T(8,128)(2,1)} %reshape.240), calls=%async_computation.3 | async-start | bytes 1048576 | tf_op jit(solution)/shard_map/all_to_all | solution.py:151
  104.9 39.4 %collective-permute-start.8 = (bf16[192,2048]{1,0:T(8,128)(2,1)}, bf16[192,2048]{1,0:T(8,128)(2,1)}, u32[]{:S(2)}, u32[]{:S(2)}) collective-permute-start(bf16[192,2048]{1,0:T(8,128)(2,1)} %get-tuple-element.18), channel_id=1, source_target_pairs={{0,16},{8,24},{16,0},{24,8},{1,17},{9,25},{17,1},{25,9},{2,18},{10... | collective-permute-start | bytes 2359304 | tf_op jit(solution)/shard_map/ppermute | solution.py:38
  129.2 40.6 %collective-permute-start.7 = (bf16[1024,768]{1,0:T(8,128)(2,1)S(1)}, bf16[1024,768]{1,0:T(8,128)(2,1)}, u32[]{:S(2)}, u32[]{:S(2)}) collective-permute-start(bf16[1024,768]{1,0:T(8,128)(2,1)S(1)} %add.114), channel_id=1, source_target_pairs={{0,8},{8,0},{16,24},{24,16},{1,9},{9,1},{17,25},{25,17},{2,10},{10... | collective-permute-start | bytes 4718600 | tf_op jit(solution)/shard_map/ppermute | solution.py:38
  132.1 14.0 %all-to-all-start.4 = ((bf16[4,2,8,2048]{3,2,1,0:T(8,128)(2,1)}), bf16[4,2,8,2048]{3,2,1,0:T(8,128)(2,1)S(1)}, u32[]{:S(2)}, u32[]{:S(2)}) async-start(bf16[4,2,8,2048]{3,2,1,0:T(8,128)(2,1)} %bitcast.78), calls=%async_computation.4 | async-start | bytes 524288 | tf_op jit(solution)/shard_map/all_to_all | solution.py:114
  145.9 8.7 %collective-permute-start.9 = (bf16[192,2048]{1,0:T(8,128)(2,1)S(1)}, bf16[192,2048]{1,0:T(8,128)(2,1)}, u32[]{:S(2)}, u32[]{:S(2)}) collective-permute-start(bf16[192,2048]{1,0:T(8,128)(2,1)S(1)} %add.116), channel_id=1, source_target_pairs={{0,8},{8,0},{16,24},{24,16},{1,9},{9,1},{17,25},{25,17},{2,10},{10... | collective-permute-start | bytes 2359304 | tf_op jit(solution)/shard_map/ppermute | solution.py:38
  148.3 21.4 %all-to-all-start.5 = ((bf16[8,10,2048]{2,1,0:T(8,128)(2,1)}), bf16[8,10,2048]{2,1,0:T(8,128)(2,1)S(1)}, u32[]{:S(2)}, u32[]{:S(2)}) async-start(bf16[8,10,2048]{2,1,0:T(8,128)(2,1)} %reshape.244), calls=%async_computation.5 | async-start | bytes 1048576 | tf_op jit(solution)/shard_map/all_to_all | solution.py:139
  (9 other events, 16.7 us)
